TPU v7x, 32 devices: a whole 2x2x4 slice. The times are simulated.
32 devices in a mesh: gy: 4 (over z), gx: 8 (over y, x, core).
Axes of the slice: x: 2, y: 2, z: 4, core: 2. Of those that a mesh axis runs over, the one named last changes fastest.
Arguments:
- tiles: bfloat16 [4096, 128, 128], P(('gy', 'gx')), may hold values from 0.19921875 to 5
- tile_dest: int32 [4096, 1], P(('gy', 'gx')), may hold values from 0 to 31, as said below
- tile_slot: int32 [4096], P(('gy', 'gx')), may hold values from 0 to 191
- psf: float32 [6, 3, 31], replicated, may hold values from 0.05 to 1
- estimate: float32 [32, 512, 1024], P(None, 'gy', 'gx'), may hold values from 0.5 to 2
Outputs:
- restored: float32 [32, 512, 1024], P(None, 'gy', 'gx')
Inputs may be any that keep to these rules, and one draw needn't show every extreme that they name: `tile_dest`: among the 128 tiles held by one device no brick is named more than 8 times; in every draw some brick is named exactly 8 times by the tiles of every device.
All inputs are finite; a program needn't handle non-finite values.
Results may differ from a plain program's by a relative error of at most 0.00069.
Values may be sent and summed in bfloat16 or wider, within the bound.
A program may use at most 192 MiB of HBM per device.

v0:
```python
import jax
import jax.numpy as jnp
from jax import lax
from jax.sharding import PartitionSpec as P

ITERS = 2


damping = 0.05


def extended(cells, sides, width):
    for axis, dim in sides:
        count = lax.axis_size(axis)
        ends = count - 1
        head = lax.slice_in_dim(cells, 0, width, axis=dim)
        tail = lax.slice_in_dim(cells, cells.shape[dim] - width, cells.shape[dim], axis=dim)
        cells = jnp.concatenate(
            [
                lax.ppermute(tail, axis, [(i, (i + 1) % count) for i in range(ends)]),
                cells,
                lax.ppermute(head, axis, [((i + 1) % count, i) for i in range(ends)]),
            ],
            axis=dim,
        )
    return cells


def banded(taps, row_count, col_count, offset_start):
    offset = jnp.arange(row_count)[:, None] - jnp.arange(col_count)[None, :] + offset_start
    picks = (offset[:, :, None] == jnp.arange(taps.shape[-1])[None, None, :]).astype(jnp.float32)
    matrix = jnp.einsum(
        "rct,vt->vrc", picks, taps.astype(jnp.float32), precision=lax.Precision.HIGHEST
    )
    return matrix.astype(jnp.bfloat16)


def local(tiles, tile_dest, tile_slot, psf, estimate):
    rows_y = lax.axis_size("gy")
    cols_x = lax.axis_size("gx")
    devices = rows_y * cols_x
    holding = tiles.shape[0]
    tile_side = tiles.shape[1]
    slot_count = 2 * ((holding + devices - 1) // devices)
    view_count = psf.shape[0]
    planes = estimate.shape[0]
    reach = (psf.shape[2] - 1) // 2
    padded_side = tile_side + 2 * reach
    target = tile_dest[:, 0]
    earlier = (target[None, :] == target[:, None]) & (
        jnp.arange(holding)[None, :] < jnp.arange(holding)[:, None]
    )
    place_rank = jnp.sum(earlier.astype(jnp.int32), axis=1)
    where_to = target * slot_count + place_rank
    placing = where_to[None, :] == jnp.arange(devices * slot_count)[:, None]
    packed = jnp.dot(
        placing.astype(jnp.bfloat16),
        tiles.reshape(holding, tile_side * tile_side),
        preferred_element_type=jnp.float32,
    ).astype(jnp.bfloat16)
    labels = jnp.sum(jnp.where(placing, tile_slot[None, :] + 1, 0), axis=1) - 1
    got_tiles, got_labels = (
        lax.all_to_all(
            packed.reshape(devices, slot_count, tile_side * tile_side),
            ("gy", "gx"),
            split_axis=0,
            concat_axis=0,
            tiled=True,
        ),
        lax.all_to_all(
            labels.reshape(devices, slot_count),
            ("gy", "gx"),
            split_axis=0,
            concat_axis=0,
            tiled=True,
        ),
    )
    got_tiles = got_tiles.reshape(-1, tile_side * tile_side)
    got_labels = got_labels.reshape(-1)
    sorting = got_labels[None, :] == jnp.arange(view_count * planes)[:, None]
    observed = jnp.dot(
        sorting.astype(jnp.bfloat16), got_tiles, preferred_element_type=jnp.float32
    ).reshape(view_count, planes, tile_side, tile_side)
    counted = jnp.sum(sorting.astype(jnp.float32), axis=1).reshape(view_count, planes)
    kernel = (psf / jnp.sum(psf, axis=2, keepdims=True)).astype(jnp.bfloat16)
    flipped = kernel[:, :, ::-1]
    band_x = banded(kernel[:, 2], padded_side, tile_side, 0)
    band_y = banded(kernel[:, 1], padded_side, tile_side, 0)
    band_z = banded(kernel[:, 0], planes, planes, reach)
    flip_x = banded(flipped[:, 2], padded_side, tile_side, 0)
    flip_y = banded(flipped[:, 1], padded_side, tile_side, 0)
    flip_z = banded(flipped[:, 0], planes, planes, reach)
    for repeat_index in range(ITERS):
        rounded = estimate.astype(jnp.bfloat16)
        widened = extended(rounded, (("gy", 1), ("gx", 2)), reach)
        along_x = jnp.einsum(
            "zyx,vxi->vzyi", widened, band_x, preferred_element_type=jnp.float32
        ).astype(jnp.bfloat16)
        along_y = jnp.einsum(
            "vzyi,vyj->vzji", along_x, band_y, preferred_element_type=jnp.float32
        ).astype(jnp.bfloat16)
        blur = jnp.einsum("vzji,vzk->vkji", along_y, band_z, preferred_element_type=jnp.float32)
        ratio = ((observed + damping) / (counted[:, :, None, None] * blur + damping)).astype(
            jnp.bfloat16
        )
        back_z = jnp.einsum(
            "vzji,vzk->vkji", ratio, flip_z, preferred_element_type=jnp.float32
        ).astype(jnp.bfloat16)
        rimmed = extended(back_z, (("gy", 2), ("gx", 3)), reach)
        back_y = jnp.einsum(
            "vzyx,vyj->vzjx", rimmed, flip_y, preferred_element_type=jnp.float32
        ).astype(jnp.bfloat16)
        correction = jnp.einsum(
            "vzjx,vxi->vzji", back_y, flip_x, preferred_element_type=jnp.float32
        )
        total = jnp.sum(correction, axis=0)
        estimate = estimate * total / view_count
    return estimate


def solution(mesh):
    placed = (
        P(("gy", "gx"), None, None),
        P(("gy", "gx"), None),
        P(("gy", "gx")),
        P(),
        P(None, "gy", "gx"),
    )
    return jax.shard_map(
        local, mesh=mesh, in_specs=placed, out_specs=P(None, "gy", "gx"), check_vma=False
    )
```

profile of v0, /device:TPU:1, one launch (start us, length us, event | category | flops | bytes accessed | tf_op | source)
XLA Modules:
  0.0 588.6 jit_solution(18207633815773273649)
XLA Ops:
  2.4 7.1 %all-to-all-start = ((s32[32,1,8]{2,1,0:T(1,128)}), s32[32,1,8]{2,1,0:T(1,128)S(1)}, u32[]{:S(2)}, u32[]{:S(2)}) async-start(s32[32,1,8]{2,1,0:T(1,128)} %bitcast.7), calls=%async_computation | async-start | bytes 32768 | tf_op jit(solution)/shard_map/all_to_all | solution.py:70
  9.5 8.9 %fusion = bf16[32,8,16384]{2,1,0:T(8,128)(2,1)} fusion(bf16[16,8,128,128]{3,2,1,0:T(8,128)(2,1)} %bitcast.134, s32[128]{0:T(128)S(1)} %get-tuple-element.26), kind=kOutput, calls=%fused_computation.1 | convolution fusion | flops 1077968896 | bytes 12583424 | tf_op jit(solution)/shard_map/dot_general | solution.py:56
  19.0 5.9 %all-to-all-start.1 = ((bf16[32,8,16384]{2,1,0:T(8,128)(2,1)}), bf16[32,8,16384]{2,1,0:T(8,128)(2,1)}, u32[]{:S(2)}, u32[]{:S(2)}) async-start(bf16[32,8,16384]{2,1,0:T(8,128)(2,1)} %fusion), calls=%async_computation.1 | async-start | bytes 16777216 | tf_op jit(solution)/shard_map/all_to_all | solution.py:63
  35.6 129.2 %collective-permute-done = bf16[32,15,128]{2,1,0:T(8,128)(2,1)S(1)} collective-permute-done((bf16[32,15,128]{2,1,0:T(8,128)(2,1)S(1)}, bf16[32,15,128]{2,1,0:T(8,128)(2,1)S(1)}, u32[]{:S(2)}, u32[]{:S(2)}) %collective-permute-start) | collective-permute-done | bytes 122912 | tf_op jit(solution)/shard_map/ppermute | solution.py:20
  183.5 7.6 %convert_bitcast_fusion.1 = bf16[6,32,128,128]{3,2,1,0:T(8,128)(2,1)} fusion(bf16[32,158,15]{2,1,0:T(8,128)(2,1)} %copy.102, bf16[32,15,128]{2,1,0:T(8,128)(2,1)} %copy-done.2, bf16[32,128,128]{2,1,0:T(8,128)(2,1)S(1)} %convert_element_type.107, bf16[32,15,128]{2,1,0:T(8,128)(2,1)S(1)} %collective-permute-done, bf16[32,158,15]{2,1,0:T(8,128)(2,1)S(1)} %copy.101, ...), kind=kOutput, calls=%fused_computation.29 | convolution fusion | flops 2236097792 | bytes 8374528 | tf_op jit(solution)/shard_map/vzyi,vyj->vzji/dot_general | solution.py:99
  191.1 19.4 %all-to-all-done.1 = bf16[32,8,16384]{2,1,0:T(8,128)(2,1)} async-done(((bf16[32,8,16384]{2,1,0:T(8,128)(2,1)}), bf16[32,8,16384]{2,1,0:T(8,128)(2,1)}, u32[]{:S(2)}, u32[]{:S(2)}) %all-to-all-start.1) | async-done | bytes 8388640 | tf_op jit(solution)/shard_map/all_to_all | solution.py:63
  210.4 11.9 %copy.95 = bf16[256,16384]{0,1:T(8,128)(2,1)} copy(bf16[256,16384]{1,0:T(8,128)(2,1)} %bitcast.11) | data formatting | bytes 16777216 | tf_op jit(solution)/shard_map/reshape | solution.py:78
  222.4 10.9 %fusion.113 = f32[6,32,128,128]{3,1,2,0:T(8,128)} fusion(bf16[128,128,256,1]{2,1,0,3:T(8,128)(2,1)} %bitcast.133, s32[6,32]{1,0:T(8,128)S(1)} %copy-done.10, s32[256]{0:T(256)S(1)} %copy-done.9), kind=kOutput, calls=%fused_computation.86 | convolution fusion | flops 1610661888 | bytes 20973312 | tf_op jit(solution)/shard_map/dot_general | solution.py:81
  233.3 13.8 %fusion.44 = bf16[6,32,128,128]{3,1,2,0:T(8,128)(2,1)} fusion(f32[6,32,128,128]{3,1,2,0:T(8,128)} %fusion.113, f32[6,32]{1,0:T(8,128)S(1)} %copy-done.7, bf16[6,32,128,128]{3,2,1,0:T(8,128)(2,1)} %convert_bitcast_fusion.1, bf16[6,32,32]{2,0,1:T(8,128)(2,1)S(1)} %copy-done.15, bf16[6,32,32]{2,0,1:T(8,128)(2,1)S(1)} %copy-done.16), kind=kOutput, calls=%fused_computation.37 | convolution fusion | flops 421527552 | bytes 25191168 | tf_op jit(solution)/shard_map/vzji,vzk->vkji/dot_general | solution.py:106
  248.7 29.2 %collective-permute-start.4 = (bf16[6,32,15,128]{3,1,2,0:T(8,128)(2,1)S(1)}, bf16[6,32,15,128]{3,1,2,0:T(8,128)(2,1)S(1)}, u32[]{:S(2)}, u32[]{:S(2)}) collective-permute-start(bf16[6,32,15,128]{3,1,2,0:T(8,128)(2,1)S(1)} %get-tuple-element.11), channel_id=1, source_target_pairs={{0,8},{8,16},{16,24},{1,9},{9,17},{17,25},{2,10},{10,18},{18,26},{... | collective-permute-start | bytes 2211848 | tf_op jit(solution)/shard_map/ppermute | solution.py:20
  279.4 14.0 %collective-permute-done.4 = bf16[6,32,15,128]{3,1,2,0:T(8,128)(2,1)S(1)} collective-permute-done((bf16[6,32,15,128]{3,1,2,0:T(8,128)(2,1)S(1)}, bf16[6,32,15,128]{3,1,2,0:T(8,128)(2,1)S(1)}, u32[]{:S(2)}, u32[]{:S(2)}) %collective-permute-start.4) | collective-permute-done | bytes 737312 | tf_op jit(solution)/shard_map/ppermute | solution.py:20
  301.5 6.7 %fusion.157 = (bf16[6,32,158,15]{3,1,2,0:T(8,128)(2,1)}, bf16[6,32,158,15]{3,1,2,0:T(8,128)(2,1)}) fusion(bf16[6,32,158,128]{3,1,2,0:T(8,128)(2,1)S(1)} %pad_maximum_fusion.2), kind=kLoop, calls=%fused_computation.123 | loop fusion | bytes 3640320 | tf_op jit(solution)/shard_map/slice | solution.py:17
  308.2 11.4 %copy.106 = bf16[6,32,158,15]{2,1,3,0:T(8,128)(2,1)S(1)} copy(bf16[6,32,158,15]{3,1,2,0:T(8,128)(2,1)} %get-tuple-element.7) | data formatting | bytes 1820160 | tf_op jit(solution)/shard_map/slice | solution.py:17
  319.6 4.4 collective-permute-start.6
  324.1 12.1 %copy.107 = bf16[6,32,158,15]{2,1,3,0:T(8,128)(2,1)} copy(bf16[6,32,158,15]{3,1,2,0:T(8,128)(2,1)} %get-tuple-element.8) | data formatting | bytes 1820160 | tf_op jit(solution)/shard_map/slice | solution.py:16
  340.4 15.8 %copy.108 = bf16[6,32,158,15]{3,1,2,0:T(8,128)(2,1)} copy(bf16[6,32,158,15]{2,1,3,0:T(8,128)(2,1)} %collective-permute-done.6) | data formatting | bytes 1820160 | tf_op jit(solution)/shard_map/ppermute | solution.py:20
  357.9 15.9 %copy.109 = bf16[6,32,158,15]{3,1,2,0:T(8,128)(2,1)} copy(bf16[6,32,158,15]{2,1,3,0:T(8,128)(2,1)} %collective-permute-done.7) | data formatting | bytes 1820160 | tf_op jit(solution)/shard_map/ppermute | solution.py:22
  373.8 19.4 %pad_maximum_fusion = bf16[6,32,158,158]{3,1,2,0:T(8,128)(2,1)} fusion(bf16[6,32,158,15]{3,1,2,0:T(8,128)(2,1)} %copy.109, bf16[6,32,15,128]{3,1,2,0:T(8,128)(2,1)S(1)} %collective-permute-done.5, bf16[6,32,128,128]{3,1,2,0:T(8,128)(2,1)} %fusion.44, bf16[6,32,15,128]{3,1,2,0:T(8,128)(2,1)S(1)} %collective-permute-done.4, bf16[6,32,158,15]{3,1,2,0:T(8,128)(2,1)} %copy.108), kind=kLoop, calls=%fused_computation.6 | loop fusion | flops 47930880 | bytes 19172352 | tf_op jit(solution)/shard_map/concatenate | solution.py:18
  393.2 16.7 %fusion.165 = (bf16[32,128,128]{2,1,0:T(8,128)(2,1)S(1)}, f32[32,128,128]{2,1,0:T(8,128)}) fusion(f32[32,128,128]{2,1,0:T(8,128)} %param.9, bf16[6,158,128]{2,0,1:T(8,128)(2,1)S(1)} %fusion.87, bf16[6,32,158,158]{3,1,2,0:T(8,128)(2,1)} %pad_maximum_fusion, bf16[6,158,128]{2,0,1:T(8,128)(2,1)S(1)} %copy-done.13), kind=kOutput, calls=%fused_computation.131 | convolution fusion | flops 2226536448 | bytes 15314432 | tf_op jit(solution)/shard_map/vzjx,vxi->vzji/dot_general | solution.py:113
  419.3 4.6 collective-permute-start.10
  427.7 5.5 collective-permute-done.11
  433.8 7.6 %convert_bitcast_fusion = bf16[6,32,128,128]{3,2,1,0:T(8,128)(2,1)} fusion(bf16[32,158,15]{2,1,0:T(8,128)(2,1)S(1)} %copy.115, bf16[32,15,128]{2,1,0:T(8,128)(2,1)S(1)} %collective-permute-done.9, bf16[32,128,128]{2,1,0:T(8,128)(2,1)} %copy-done.1, bf16[32,15,128]{2,1,0:T(8,128)(2,1)S(1)} %collective-permute-done.8, bf16[32,158,15]{2,1,0:T(8,128)(2,1)S(1)} %copy.114, ...), kind=kOutput, calls=%fused_computation.28 | convolution fusion | flops 2236097792 | bytes 8374528 | tf_op jit(solution)/shard_map/vzyi,vyj->vzji/dot_general | solution.py:99
  441.4 13.9 %fusion.41 = bf16[6,32,128,128]{3,1,2,0:T(8,128)(2,1)} fusion(f32[6,32,128,128]{3,1,2,0:T(8,128)} %fusion.113, f32[6,32]{1,0:T(8,128)S(1)} %copy-done.7, bf16[6,32,128,128]{3,2,1,0:T(8,128)(2,1)} %convert_bitcast_fusion, bf16[6,32,32]{2,0,1:T(8,128)(2,1)S(1)} %copy-done.15, bf16[6,32,32]{2,0,1:T(8,128)(2,1)S(1)} %copy-done.17), kind=kOutput, calls=%fused_computation.36 | convolution fusion | flops 421527552 | bytes 25191168 | tf_op jit(solution)/shard_map/vzji,vzk->vkji/dot_general | solution.py:106
  460.3 9.8 %collective-permute-done.12 = bf16[6,32,15,128]{3,1,2,0:T(8,128)(2,1)S(1)} collective-permute-done((bf16[6,32,15,128]{3,1,2,0:T(8,128)(2,1)S(1)}, bf16[6,32,15,128]{3,1,2,0:T(8,128)(2,1)S(1)}, u32[]{:S(2)}, u32[]{:S(2)}) %collective-permute-start.12) | collective-permute-done | bytes 737312 | tf_op jit(solution)/shard_map/ppermute | solution.py:20
  478.1 6.7 %fusion.156 = (bf16[6,32,158,15]{3,1,2,0:T(8,128)(2,1)}, bf16[6,32,158,15]{3,1,2,0:T(8,128)(2,1)}) fusion(bf16[6,32,158,128]{3,1,2,0:T(8,128)(2,1)S(1)} %pad_maximum_fusion.3), kind=kLoop, calls=%fused_computation.122 | loop fusion | bytes 3640320 | tf_op jit(solution)/shard_map/slice | solution.py:17
  484.8 11.4 %copy.119 = bf16[6,32,158,15]{2,1,3,0:T(8,128)(2,1)S(1)} copy(bf16[6,32,158,15]{3,1,2,0:T(8,128)(2,1)} %get-tuple-element.5) | data formatting | bytes 1820160 | tf_op jit(solution)/shard_map/slice | solution.py:17
  496.2 5.7 collective-permute-start.14
  501.9 12.1 %copy.120 = bf16[6,32,158,15]{2,1,3,0:T(8,128)(2,1)} copy(bf16[6,32,158,15]{3,1,2,0:T(8,128)(2,1)} %get-tuple-element.6) | data formatting | bytes 1820160 | tf_op jit(solution)/shard_map/slice | solution.py:16
  518.2 15.8 %copy.121 = bf16[6,32,158,15]{3,1,2,0:T(8,128)(2,1)} copy(bf16[6,32,158,15]{2,1,3,0:T(8,128)(2,1)} %collective-permute-done.14) | data formatting | bytes 1820160 | tf_op jit(solution)/shard_map/ppermute | solution.py:20
  536.4 15.8 %copy.122 = bf16[6,32,158,15]{3,1,2,0:T(8,128)(2,1)} copy(bf16[6,32,158,15]{2,1,3,0:T(8,128)(2,1)} %collective-permute-done.15) | data formatting | bytes 1820160 | tf_op jit(solution)/shard_map/ppermute | solution.py:22
  552.2 19.4 %pad_maximum_fusion.1 = bf16[6,32,158,158]{3,1,2,0:T(8,128)(2,1)} fusion(bf16[6,32,158,15]{3,1,2,0:T(8,128)(2,1)} %copy.122, bf16[6,32,15,128]{3,1,2,0:T(8,128)(2,1)S(1)} %collective-permute-done.13, bf16[6,32,128,128]{3,1,2,0:T(8,128)(2,1)} %fusion.41, bf16[6,32,15,128]{3,1,2,0:T(8,128)(2,1)S(1)} %collective-permute-done.12, bf16[6,32,158,15]{3,1,2,0:T(8,128)(2,1)} %copy.121), kind=kLoop, calls=%fused_computation.7 | loop fusion | flops 47930880 | bytes 19172352 | tf_op jit(solution)/shard_map/concatenate | solution.py:18
  571.7 16.7 %fusion.91 = f32[32,128,128]{2,1,0:T(8,128)} fusion(f32[32,128,128]{2,1,0:T(8,128)} %get-tuple-element.25, bf16[6,32,158,158]{3,1,2,0:T(8,128)(2,1)} %pad_maximum_fusion.1, bf16[6,158,128]{2,0,1:T(8,128)(2,1)S(1)} %copy-done.12, bf16[6,158,128]{2,0,1:T(8,128)(2,1)S(1)} %copy-done.14), kind=kOutput, calls=%fused_computation.62 | convolution fusion | flops 2226012160 | bytes 14265856 | tf_op jit(solution)/shard_map/vzjx,vxi->vzji/dot_general | solution.py:113
  (106 shorter events, 82.5 us)
Async XLA Ops:
  2.4 16.0 %all-to-all-start = ((s32[32,1,8]{2,1,0:T(1,128)}), s32[32,1,8]{2,1,0:T(1,128)S(1)}, u32[]{:S(2)}, u32[]{:S(2)}) async-start(s32[32,1,8]{2,1,0:T(1,128)} %bitcast.7), calls=%async_computation | async-start | bytes 32768 | tf_op jit(solution)/shard_map/all_to_all | solution.py:70
  18.4 11.3 %copy-start.4 = (f32[6,3,31]{2,1,0:T(4,128)S(1)}, f32[6,3,31]{2,1,0:T(4,128)}, u32[]{:S(2)}) copy-start(f32[6,3,31]{2,1,0:T(4,128)} %param.8) | copy-start | bytes 6700
  19.0 191.4 %all-to-all-start.1 = ((bf16[32,8,16384]{2,1,0:T(8,128)(2,1)}), bf16[32,8,16384]{2,1,0:T(8,128)(2,1)}, u32[]{:S(2)}, u32[]{:S(2)}) async-start(bf16[32,8,16384]{2,1,0:T(8,128)(2,1)} %fusion), calls=%async_computation.1 | async-start | bytes 16777216 | tf_op jit(solution)/shard_map/all_to_all | solution.py:63
  25.2 139.6 %collective-permute-start = (bf16[32,15,128]{2,1,0:T(8,128)(2,1)S(1)}, bf16[32,15,128]{2,1,0:T(8,128)(2,1)S(1)}, u32[]{:S(2)}, u32[]{:S(2)}) collective-permute-start(bf16[32,15,128]{2,1,0:T(8,128)(2,1)S(1)} %get-tuple-element.19), channel_id=1, source_target_pairs={{0,8},{8,16},{16,24},{1,9},{9,17},{17,25},{2,10},{10,18},{18,26},{... | collective-permute-start | bytes 368648 | tf_op jit(solution)/shard_map/ppermute | solution.py:20
  28.5 136.3 %collective-permute-start.1 = (bf16[32,15,128]{2,1,0:T(8,128)(2,1)S(1)}, bf16[32,15,128]{2,1,0:T(8,128)(2,1)S(1)}, u32[]{:S(2)}, u32[]{:S(2)}) collective-permute-start(bf16[32,15,128]{2,1,0:T(8,128)(2,1)S(1)} %get-tuple-element.20), channel_id=1, source_target_pairs={{8,0},{16,8},{24,16},{9,1},{17,9},{25,17},{10,2},{18,10},{26,18},{... | collective-permute-start | bytes 368648 | tf_op jit(solution)/shard_map/ppermute | solution.py:22
  169.4 9.9 %collective-permute-start.2 = (bf16[32,158,15]{1,0,2:T(8,128)(2,1)S(1)}, bf16[32,158,15]{1,0,2:T(8,128)(2,1)S(1)}, u32[]{:S(2)}, u32[]{:S(2)}) collective-permute-start(bf16[32,158,15]{1,0,2:T(8,128)(2,1)S(1)} %copy.99), channel_id=1, source_target_pairs={{0,1},{1,2},{2,3},{3,4},{4,5},{5,6},{6,7},{8,9},{9,10},{10,11},{11... | collective-permute-start | bytes 455048 | tf_op jit(solution)/shard_map/ppermute | solution.py:20
  173.6 8.3 %collective-permute-start.3 = (bf16[32,158,15]{1,0,2:T(8,128)(2,1)S(1)}, bf16[32,158,15]{1,0,2:T(8,128)(2,1)S(1)}, u32[]{:S(2)}, u32[]{:S(2)}) collective-permute-start(bf16[32,158,15]{1,0,2:T(8,128)(2,1)S(1)} %copy.100), channel_id=1, source_target_pairs={{1,0},{2,1},{3,2},{4,3},{5,4},{6,5},{7,6},{9,8},{10,9},{11,10},{12... | collective-permute-start | bytes 455048 | tf_op jit(solution)/shard_map/ppermute | solution.py:22
  210.4 11.9 %copy-start.9 = (s32[256]{0:T(256)S(1)}, s32[256]{0:T(256)}, u32[]{:S(2)}) copy-start(s32[256]{0:T(256)} %copy-done.8) | copy-start | bytes 3076
  210.4 11.9 %copy-start.10 = (s32[6,32]{1,0:T(8,128)S(1)}, s32[6,32]{1,0:T(8,128)}, u32[]{:S(2)}) copy-start(s32[6,32]{1,0:T(8,128)} %multiply_add_fusion) | copy-start | bytes 2308
  222.4 10.9 %copy-start.7 = (f32[6,32]{1,0:T(8,128)S(1)}, f32[6,32]{1,0:T(8,128)}, u32[]{:S(2)}) copy-start(f32[6,32]{1,0:T(8,128)} %mul.34) | copy-start | bytes 2308
  222.4 10.9 %copy-start.15 = (bf16[6,32,32]{2,0,1:T(8,128)(2,1)S(1)}, bf16[6,32,32]{2,0,1:T(8,128)(2,1)}, u32[]{:S(2)}) copy-start(bf16[6,32,32]{2,0,1:T(8,128)(2,1)} %fusion.105) | copy-start | bytes 36868
  222.4 10.9 %copy-start.16 = (bf16[6,32,32]{2,0,1:T(8,128)(2,1)S(1)}, bf16[6,32,32]{2,0,1:T(8,128)(2,1)}, u32[]{:S(2)}) copy-start(bf16[6,32,32]{2,0,1:T(8,128)(2,1)} %fusion.106) | copy-start | bytes 36868
  248.7 44.7 %collective-permute-start.4 = (bf16[6,32,15,128]{3,1,2,0:T(8,128)(2,1)S(1)}, bf16[6,32,15,128]{3,1,2,0:T(8,128)(2,1)S(1)}, u32[]{:S(2)}, u32[]{:S(2)}) collective-permute-start(bf16[6,32,15,128]{3,1,2,0:T(8,128)(2,1)S(1)} %get-tuple-element.11), channel_id=1, source_target_pairs={{0,8},{8,16},{16,24},{1,9},{9,17},{17,25},{2,10},{10,18},{18,26},{... | collective-permute-start | bytes 2211848 | tf_op jit(solution)/shard_map/ppermute | solution.py:20
  277.9 19.7 %collective-permute-start.5 = (bf16[6,32,15,128]{3,1,2,0:T(8,128)(2,1)S(1)}, bf16[6,32,15,128]{3,1,2,0:T(8,128)(2,1)S(1)}, u32[]{:S(2)}, u32[]{:S(2)}) collective-permute-start(bf16[6,32,15,128]{3,1,2,0:T(8,128)(2,1)S(1)} %get-tuple-element.12), channel_id=1, source_target_pairs={{8,0},{16,8},{24,16},{9,1},{17,9},{25,17},{10,2},{18,10},{26,18},{... | collective-permute-start | bytes 2211848 | tf_op jit(solution)/shard_map/ppermute | solution.py:22
  319.6 18.5 %copy-start.6 = (bf16[6,1,31]{2,0,1:T(8,128)(2,1)S(1)}, bf16[6,1,31]{2,0,1:T(8,128)(2,1)}, u32[]{:S(2)}) copy-start(bf16[6,1,31]{2,0,1:T(8,128)(2,1)} %get-tuple-element.22) | copy-start | bytes 1120
  319.6 18.6 %copy-start.5 = (bf16[6,1,31]{2,0,1:T(8,128)(2,1)S(1)}, bf16[6,1,31]{2,0,1:T(8,128)(2,1)}, u32[]{:S(2)}) copy-start(bf16[6,1,31]{2,0,1:T(8,128)(2,1)} %get-tuple-element.21) | copy-start | bytes 1120
  319.6 20.7 %collective-permute-start.6 = (bf16[6,32,158,15]{2,1,3,0:T(8,128)(2,1)S(1)}, bf16[6,32,158,15]{2,1,3,0:T(8,128)(2,1)}, u32[]{:S(2)}, u32[]{:S(2)}) collective-permute-start(bf16[6,32,158,15]{2,1,3,0:T(8,128)(2,1)S(1)} %copy.106), channel_id=1, source_target_pairs={{0,1},{1,2},{2,3},{3,4},{4,5},{5,6},{6,7},{8,9},{9,10},{10,11},{11... | collective-permute-start | bytes 2730248 | tf_op jit(solution)/shard_map/ppermute | solution.py:20
  336.2 21.7 %collective-permute-start.7 = (bf16[6,32,158,15]{2,1,3,0:T(8,128)(2,1)}, bf16[6,32,158,15]{2,1,3,0:T(8,128)(2,1)}, u32[]{:S(2)}, u32[]{:S(2)}) collective-permute-start(bf16[6,32,158,15]{2,1,3,0:T(8,128)(2,1)} %copy.107), channel_id=1, source_target_pairs={{1,0},{2,1},{3,2},{4,3},{5,4},{6,5},{7,6},{9,8},{10,9},{11,10},{12... | collective-permute-start | bytes 2730248 | tf_op jit(solution)/shard_map/ppermute | solution.py:22
  338.8 54.4 %copy-start.11 = (bf16[6,158,128]{2,0,1:T(8,128)(2,1)}, bf16[6,158,128]{2,0,1:T(8,128)(2,1)S(1)}, u32[]{:S(2)}) copy-start(bf16[6,158,128]{2,0,1:T(8,128)(2,1)S(1)} %fusion.87) | copy-start | bytes 728068
  373.8 19.4 %copy-start.13 = (bf16[6,158,128]{2,0,1:T(8,128)(2,1)S(1)}, bf16[6,158,128]{2,0,1:T(8,128)(2,1)}, u32[]{:S(2)}) copy-start(bf16[6,158,128]{2,0,1:T(8,128)(2,1)} %fusion.90) | copy-start | bytes 728068
  409.9 7.7 %copy-start.1 = (bf16[32,128,128]{2,1,0:T(8,128)(2,1)}, bf16[32,128,128]{2,1,0:T(8,128)(2,1)S(1)}, u32[]{:S(2)}) copy-start(bf16[32,128,128]{2,1,0:T(8,128)(2,1)S(1)} %get-tuple-element.24) | copy-start | bytes 3145732
  410.0 3.8 collective-permute-start.8
  411.9 5.7 collective-permute-start.9
  419.3 7.7 %collective-permute-start.10 = (bf16[32,158,15]{1,0,2:T(8,128)(2,1)S(1)}, bf16[32,158,15]{1,0,2:T(8,128)(2,1)S(1)}, u32[]{:S(2)}, u32[]{:S(2)}) collective-permute-start(bf16[32,158,15]{1,0,2:T(8,128)(2,1)S(1)} %copy.112), channel_id=1, source_target_pairs={{0,1},{1,2},{2,3},{3,4},{4,5},{5,6},{6,7},{8,9},{9,10},{10,11},{11... | collective-permute-start | bytes 455048 | tf_op jit(solution)/shard_map/ppermute | solution.py:20
  424.8 8.4 %collective-permute-start.11 = (bf16[32,158,15]{1,0,2:T(8,128)(2,1)S(1)}, bf16[32,158,15]{1,0,2:T(8,128)(2,1)S(1)}, u32[]{:S(2)}, u32[]{:S(2)}) collective-permute-start(bf16[32,158,15]{1,0,2:T(8,128)(2,1)S(1)} %copy.113), channel_id=1, source_target_pairs={{1,0},{2,1},{3,2},{4,3},{5,4},{6,5},{7,6},{9,8},{10,9},{11,10},{12... | collective-permute-start | bytes 455048 | tf_op jit(solution)/shard_map/ppermute | solution.py:22
  433.8 7.6 %copy-start.17 = (bf16[6,32,32]{2,0,1:T(8,128)(2,1)S(1)}, bf16[6,32,32]{2,0,1:T(8,128)(2,1)}, u32[]{:S(2)}) copy-start(bf16[6,32,32]{2,0,1:T(8,128)(2,1)} %fusion.106) | copy-start | bytes 36868
  457.0 13.1 %collective-permute-start.12 = (bf16[6,32,15,128]{3,1,2,0:T(8,128)(2,1)S(1)}, bf16[6,32,15,128]{3,1,2,0:T(8,128)(2,1)S(1)}, u32[]{:S(2)}, u32[]{:S(2)}) collective-permute-start(bf16[6,32,15,128]{3,1,2,0:T(8,128)(2,1)S(1)} %get-tuple-element.9), channel_id=1, source_target_pairs={{0,8},{8,16},{16,24},{1,9},{9,17},{17,25},{2,10},{10,18},{18,26},{... | collective-permute-start | bytes 2211848 | tf_op jit(solution)/shard_map/ppermute | solution.py:20
  459.0 15.2 %collective-permute-start.13 = (bf16[6,32,15,128]{3,1,2,0:T(8,128)(2,1)S(1)}, bf16[6,32,15,128]{3,1,2,0:T(8,128)(2,1)S(1)}, u32[]{:S(2)}, u32[]{:S(2)}) collective-permute-start(bf16[6,32,15,128]{3,1,2,0:T(8,128)(2,1)S(1)} %get-tuple-element.10), channel_id=1, source_target_pairs={{8,0},{16,8},{24,16},{9,1},{17,9},{25,17},{10,2},{18,10},{26,18},{... | collective-permute-start | bytes 2211848 | tf_op jit(solution)/shard_map/ppermute | solution.py:22
  496.2 22.0 %collective-permute-start.14 = (bf16[6,32,158,15]{2,1,3,0:T(8,128)(2,1)S(1)}, bf16[6,32,158,15]{2,1,3,0:T(8,128)(2,1)}, u32[]{:S(2)}, u32[]{:S(2)}) collective-permute-start(bf16[6,32,158,15]{2,1,3,0:T(8,128)(2,1)S(1)} %copy.119), channel_id=1, source_target_pairs={{0,1},{1,2},{2,3},{3,4},{4,5},{5,6},{6,7},{8,9},{9,10},{10,11},{11... | collective-permute-start | bytes 2730248 | tf_op jit(solution)/shard_map/ppermute | solution.py:20
  514.0 22.4 %collective-permute-start.15 = (bf16[6,32,158,15]{2,1,3,0:T(8,128)(2,1)}, bf16[6,32,158,15]{2,1,3,0:T(8,128)(2,1)}, u32[]{:S(2)}, u32[]{:S(2)}) collective-permute-start(bf16[6,32,158,15]{2,1,3,0:T(8,128)(2,1)} %copy.120), channel_id=1, source_target_pairs={{1,0},{2,1},{3,2},{4,3},{5,4},{6,5},{7,6},{9,8},{10,9},{11,10},{12... | collective-permute-start | bytes 2730248 | tf_op jit(solution)/shard_map/ppermute | solution.py:22
  552.2 19.4 %copy-start.12 = (bf16[6,158,128]{2,0,1:T(8,128)(2,1)S(1)}, bf16[6,158,128]{2,0,1:T(8,128)(2,1)}, u32[]{:S(2)}) copy-start(bf16[6,158,128]{2,0,1:T(8,128)(2,1)} %copy-done.11) | copy-start | bytes 728068
  552.2 19.4 %copy-start.14 = (bf16[6,158,128]{2,0,1:T(8,128)(2,1)S(1)}, bf16[6,158,128]{2,0,1:T(8,128)(2,1)}, u32[]{:S(2)}) copy-start(bf16[6,158,128]{2,0,1:T(8,128)(2,1)} %fusion.90) | copy-start | bytes 728068
  (4 other events, 8.6 us)
where the time goes:
time: 596 us; the launch traced here: 589 us
  waiting for transfers between devices  199 us (33%)
  local copies, waits for them, and re-layouts  153 us (26%)
  matrix products  103 us (17%)
  starting transfers between devices  81.4 us (14%)
  other arithmetic  51.6 us (9%)
    ppermute x8, waiting for transfers between devices, extended(): lax.ppermute(tail, axis, [(i, (i + 1) % count) for i in range(ends)])  156 us
    ppermute x8, starting transfers between devices, extended(): lax.ppermute(tail, axis, [(i, (i + 1) % count) for i in range(ends)])  54.4 us
    concatenate x6, other arithmetic, extended(): jnp.concatenate([lax.ppermute(tail, axis, [(i, (i + 1) % count) for i in...  47.5 us
    slice x12, local copies, waits for them, and re-layouts, extended(): lax.slice_in_dim(cells, cells.shape[dim] - width, cells.shape[dim], axis=...  44.5 us
    ppermute x4, local copies, waits for them, and re-layouts, extended(): lax.ppermute(head, axis, [((i + 1) % count, i) for i in range(ends)])  34 us
    dot_general x2, matrix products, local(): jnp.einsum('vzjx,vxi->vzji', back_y, flip_x, preferred_element_type=jnp.f...  33.5 us
    ppermute x4, local copies, waits for them, and re-layouts, extended(): lax.ppermute(tail, axis, [(i, (i + 1) % count) for i in range(ends)])  32.9 us
    dot_general x2, matrix products, local(): jnp.einsum('vzji,vzk->vkji', ratio, flip_z, preferred_element_type=jnp.fl...  27.7 us
  transfers between devices with their start and end apart: 18, of which 15 were waited for; matrix products, arithmetic and copies ran while one was open for 16% of the time, Pallas kernels for 0%

commit v1 on v0

v1 whole, which is shorter than its diff:
```python
import functools

import jax
import jax.numpy as jnp
from jax import lax
from jax.experimental import pallas as pl
from jax.experimental.pallas import tpu as pltpu
from jax.sharding import PartitionSpec as P

ITERS = 2
PAD = 16
VMEM = 56 * 1024 * 1024

damping = 0.05


def coordinate(index, side):
    return jnp.where(index < side, index, jnp.where(index < side + PAD, index - side - PAD, index - PAD))


def toeplitz(taps_ref, row, offset):
    def add(t, held):
        return jnp.where(offset == t, taps_ref[row, t], held)

    return lax.fori_loop(0, taps_ref.shape[1], add, jnp.zeros(offset.shape, jnp.float32))


def bands_kernel(reach, planes, side, taps_ref, bx_ref, by_ref, kz_ref, kf_ref, fy_ref, fx_ref):
    views = by_ref.shape[0]
    ext = side + 2 * PAD
    wide = fx_ref.shape[1]
    iota = lambda shape, dim: lax.broadcasted_iota(jnp.int32, shape, dim)
    tall_off = coordinate(iota((ext, side), 0), side) - iota((ext, side), 1) + reach
    long_ext = iota((side, wide), 1)
    long_off = coordinate(long_ext, side) - iota((side, wide), 0) + reach
    long_off = jnp.where(long_ext < ext, long_off, -1)
    lanes = 128
    z_col = iota((planes, lanes), 1)
    z_diff = z_col - iota((planes, lanes), 0)
    full = planes * 8
    spread_l = (iota((full, planes), 0) // 8 == iota((full, planes), 1)).astype(jnp.bfloat16)
    spread_r = (iota((lanes, full), 1) // 8 == iota((lanes, full), 0)).astype(jnp.bfloat16)
    same = iota((full, full), 0) % 8 == iota((full, full), 1) % 8

    def kron(row, offset):
        small = toeplitz(taps_ref, row, offset).astype(jnp.bfloat16)
        right = jnp.dot(small, spread_r, preferred_element_type=jnp.float32).astype(jnp.bfloat16)
        both = jnp.dot(spread_l, right, preferred_element_type=jnp.float32)
        return jnp.where(same, both, 0.0).astype(jnp.bfloat16)

    for v in range(views):
        kz_ref[v] = kron(3 * v, jnp.where(z_col < planes, z_diff + reach, -1))
        kf_ref[v] = kron(3 * v, jnp.where(z_col < planes, reach - z_diff, -1))
        tall_y = toeplitz(taps_ref, 3 * v + 1, tall_off)
        long_y = toeplitz(taps_ref, 3 * v + 1, long_off)
        fy_ref[v] = tall_y.astype(jnp.bfloat16)
        by_ref[v] = long_y[:, :ext].astype(jnp.bfloat16)
        tall_x = toeplitz(taps_ref, 3 * v + 2, tall_off)
        long_x = toeplitz(taps_ref, 3 * v + 2, long_off)
        bx_ref[:, v * side : (v + 1) * side] = tall_x.astype(jnp.bfloat16)
        fx_ref[v * side : (v + 1) * side, :] = long_x.astype(jnp.bfloat16)


def bands(taps, planes, side):
    views = taps.shape[0] // 3
    ext = side + 2 * PAD
    shapes = [
        (ext, views * side),
        (views, side, ext),
        (views, planes * 8, planes * 8),
        (views, planes * 8, planes * 8),
        (views, ext, side),
        (views * side, 2 * side),
    ]
    return pl.pallas_call(
        functools.partial(bands_kernel, (taps.shape[1] - 1) // 2, planes, side),
        out_shape=[jax.ShapeDtypeStruct(s, jnp.bfloat16) for s in shapes],
        in_specs=[pl.BlockSpec(memory_space=pltpu.SMEM)],
        out_specs=[pl.BlockSpec(memory_space=pltpu.VMEM)] * len(shapes),
        compiler_params=pltpu.CompilerParams(vmem_limit_bytes=VMEM),
        name="bands",
    )(taps)


def pack_kernel(pick_ref, tiles_ref, out_ref, sem):
    count = out_ref.shape[0]

    def send(slot, carry):
        pltpu.make_async_copy(tiles_ref.at[pick_ref[slot]], out_ref.at[slot], sem).start()
        return carry

    lax.fori_loop(0, count, send, 0)
    pltpu.make_async_copy(out_ref, out_ref, sem).wait()


def pack(pick, tiles):
    count = pick.shape[0]
    return pl.pallas_call(
        pack_kernel,
        out_shape=jax.ShapeDtypeStruct((count,) + tiles.shape[1:], tiles.dtype),
        in_specs=[pl.BlockSpec(memory_space=pltpu.SMEM), pl.BlockSpec(memory_space=pltpu.VMEM)],
        out_specs=pl.BlockSpec(memory_space=pl.ANY),
        scratch_shapes=[pltpu.SemaphoreType.DMA],
        compiler_params=pltpu.CompilerParams(vmem_limit_bytes=VMEM),
        name="pack",
    )(pick, tiles)


def observe_kernel(chunk, label_ref, tiles_ref, out_ref):
    step = pl.program_id(0)

    @pl.when(step == 0)
    def _():
        def clear(plane, carry):
            out_ref[plane] = jnp.zeros(out_ref.shape[1:], out_ref.dtype)
            return carry

        lax.fori_loop(0, out_ref.shape[0], clear, 0)

    def add(i, carry):
        label = label_ref[step * chunk + i]

        @pl.when(label >= 0)
        def _():
            out_ref[label] += tiles_ref[i].astype(jnp.float32)

        return carry

    lax.fori_loop(0, chunk, add, 0)


def observe(labels, tiles, slots):
    chunk = 32
    side = tiles.shape[1]
    return pl.pallas_call(
        functools.partial(observe_kernel, chunk),
        out_shape=jax.ShapeDtypeStruct((slots, side, side), jnp.float32),
        grid=(tiles.shape[0] // chunk,),
        in_specs=[
            pl.BlockSpec(memory_space=pltpu.SMEM),
            pl.BlockSpec((chunk, side, side), lambda i: (i, 0, 0)),
        ],
        out_specs=pl.BlockSpec((slots, side, side), lambda i: (0, 0, 0)),
        compiler_params=pltpu.CompilerParams(vmem_limit_bytes=VMEM),
        name="observe",
    )(labels, tiles)


def sides_kernel(wide_ref, bx_ref, by_ref, out_ref):
    views, planes, side, _ = out_ref.shape
    for z in range(planes):
        along_x = jnp.dot(wide_ref[z], bx_ref[...], preferred_element_type=jnp.float32).astype(jnp.bfloat16)
        for v in range(views):
            out_ref[v, z] = jnp.dot(
                by_ref[v], along_x[:, v * side : (v + 1) * side], preferred_element_type=jnp.float32
            ).astype(jnp.bfloat16)


def sides(wide, bx, by):
    planes, ext, _ = wide.shape
    views, side, _ = by.shape
    chunk = 4
    macs = planes * ext * ext * side * views + planes * views * side * side * ext
    return pl.pallas_call(
        sides_kernel,
        out_shape=jax.ShapeDtypeStruct((views, planes, side, side), jnp.bfloat16),
        grid=(planes // chunk,),
        in_specs=[
            pl.BlockSpec((chunk, ext, ext), lambda i: (i, 0, 0)),
            pl.BlockSpec(bx.shape, lambda i: (0, 0)),
            pl.BlockSpec(by.shape, lambda i: (0, 0, 0)),
        ],
        out_specs=pl.BlockSpec((views, chunk, side, side), lambda i: (0, i, 0, 0)),
        compiler_params=pltpu.CompilerParams(vmem_limit_bytes=VMEM),
        cost_estimate=pl.CostEstimate(flops=2 * macs, bytes_accessed=views * planes * side * side * 3, transcendentals=0),
        name="sides",
    )(wide, bx, by)


def depth_kernel(sides_ref, seen_ref, count_ref, kz_ref, kf_ref, out_ref):
    _, planes, rows, side = sides_ref.shape
    full = planes * 8
    pairs = rows // 16
    count = jnp.broadcast_to(count_ref[0][:, None, :], (planes, 8, side)).reshape(full, side)
    count = jnp.concatenate([count, count], axis=1)

    def both(values):
        return jnp.concatenate([values[:, :8].reshape(full, side), values[:, 8:].reshape(full, side)], axis=1)

    for p in range(pairs):
        spot = slice(p * 16, p * 16 + 16)
        stack = both(sides_ref[0, :, spot].astype(jnp.float32)).astype(jnp.bfloat16)
        blur = jnp.dot(kz_ref[0], stack, preferred_element_type=jnp.float32)
        seen = both(seen_ref[0, :, spot].astype(jnp.float32))
        ratio = ((seen + damping) / (count * blur + damping)).astype(jnp.bfloat16)
        back = jnp.dot(kf_ref[0], ratio, preferred_element_type=jnp.float32)
        out_ref[0, :, spot] = jnp.concatenate(
            [back[:, :side].reshape(planes, 8, side), back[:, side:].reshape(planes, 8, side)], axis=1
        ).astype(jnp.bfloat16)


def depth(along, seen, count, kz, kf):
    views, planes, side, _ = along.shape
    rows = 128
    block = pl.BlockSpec((1, planes, rows, side), lambda v, i: (v, 0, i, 0))
    per_view = lambda a: pl.BlockSpec((1,) + a.shape[1:], lambda v, i: (v,) + (0,) * (a.ndim - 1))
    return pl.pallas_call(
        depth_kernel,
        out_shape=jax.ShapeDtypeStruct(along.shape, jnp.bfloat16),
        grid=(views, side // rows),
        in_specs=[block, block, per_view(count), per_view(kz), per_view(kf)],
        out_specs=block,
        compiler_params=pltpu.CompilerParams(vmem_limit_bytes=VMEM),
        name="depth",
    )(along, seen, count, kz, kf)


def spread_kernel(back_ref, fy_ref, fx_ref, out_ref):
    views, planes, _, _ = back_ref.shape
    for z in range(planes):
        wide = jnp.concatenate(
            [
                jnp.dot(fy_ref[v], back_ref[v, z], preferred_element_type=jnp.float32).astype(jnp.bfloat16)
                for v in range(views)
            ],
            axis=1,
        )
        out_ref[z] = jnp.dot(wide, fx_ref[...], preferred_element_type=jnp.float32)


def spread(back, fy, fx):
    views, planes, side, _ = back.shape
    ext = fy.shape[1]
    chunk = 4
    return pl.pallas_call(
        spread_kernel,
        out_shape=jax.ShapeDtypeStruct((planes, ext, fx.shape[1]), jnp.float32),
        grid=(planes // chunk,),
        in_specs=[
            pl.BlockSpec((views, chunk, side, side), lambda i: (0, i, 0, 0)),
            pl.BlockSpec(fy.shape, lambda i: (0, 0, 0)),
            pl.BlockSpec(fx.shape, lambda i: (0, 0)),
        ],
        out_specs=pl.BlockSpec((chunk, ext, fx.shape[1]), lambda i: (i, 0, 0)),
        compiler_params=pltpu.CompilerParams(vmem_limit_bytes=VMEM),
        name="spread",
    )(back, fy, fx)


def shift(values, axis, way):
    count = lax.axis_size(axis)
    pairs = [(i, i + 1) for i in range(count - 1)]
    return lax.ppermute(values, axis, pairs if way > 0 else [(b, a) for a, b in pairs])


def widened(estimate):
    cells = estimate.astype(jnp.bfloat16)
    for axis, dim in (("gy", 1), ("gx", 2)):
        side = cells.shape[dim]
        head = lax.slice_in_dim(cells, 0, PAD, axis=dim)
        tail = lax.slice_in_dim(cells, side - PAD, side, axis=dim)
        cells = jnp.concatenate([cells, shift(tail, axis, 1), shift(head, axis, -1)], axis=dim)
    return cells


def gathered(partial, side):
    ext = side + 2 * PAD
    total = partial
    for axis, dim in (("gy", 1), ("gx", 2)):
        before = lax.slice_in_dim(total, side, side + PAD, axis=dim).astype(jnp.bfloat16)
        after = lax.slice_in_dim(total, side + PAD, ext, axis=dim).astype(jnp.bfloat16)
        to_tail = shift(before, axis, -1).astype(jnp.float32)
        to_head = shift(after, axis, 1).astype(jnp.float32)
        inner = lax.slice_in_dim(total, 0, side, axis=dim)
        total = jnp.concatenate(
            [
                lax.slice_in_dim(inner, 0, PAD, axis=dim) + to_head,
                lax.slice_in_dim(inner, PAD, side - PAD, axis=dim),
                lax.slice_in_dim(inner, side - PAD, side, axis=dim) + to_tail,
            ],
            axis=dim,
        )
    return total


def local(tiles, tile_dest, tile_slot, psf, estimate):
    devices = lax.axis_size("gy") * lax.axis_size("gx")
    holding, side, _ = tiles.shape
    slot_count = 2 * ((holding + devices - 1) // devices)
    views, _, taps = psf.shape
    planes = estimate.shape[0]
    target = tile_dest[:, 0]
    earlier = (target[None, :] == target[:, None]) & (
        jnp.arange(holding)[None, :] < jnp.arange(holding)[:, None]
    )
    rank = jnp.sum(earlier.astype(jnp.int32), axis=1)
    where_to = target * slot_count + rank
    placing = where_to[None, :] == jnp.arange(devices * slot_count)[:, None]
    pick = jnp.sum(jnp.where(placing, jnp.arange(holding, dtype=jnp.int32)[None, :], 0), axis=1)
    labels = jnp.sum(jnp.where(placing, tile_slot[None, :] + 1, 0), axis=1) - 1
    packed = pack(pick, tiles)
    exchange = functools.partial(
        lax.all_to_all, axis_name=("gy", "gx"), split_axis=0, concat_axis=0, tiled=True
    )
    got_labels = exchange(labels.reshape(devices, slot_count)).reshape(-1)
    got_tiles = exchange(packed.reshape(devices, slot_count, side, side)).reshape(-1, side, side)

    kernel = (psf / jnp.sum(psf, axis=2, keepdims=True)).astype(jnp.bfloat16).astype(jnp.float32)
    bx, by, kz, kf, fy, fx = bands(kernel.reshape(views * 3, taps), planes, side)
    along = sides(widened(estimate), bx, by)

    seen = observe(got_labels, got_tiles, views * planes).reshape(views, planes, side, side)
    sorting = got_labels[None, :] == jnp.arange(views * planes)[:, None]
    counted = jnp.sum(sorting.astype(jnp.float32), axis=1).reshape(views, planes)
    count = jnp.broadcast_to(counted[:, :, None], (views, planes, side))
    for repeat_index in range(ITERS):
        if repeat_index:
            along = sides(widened(estimate), bx, by)
        back = depth(along, seen, count, kz, kf)
        estimate = estimate * gathered(spread(back, fy, fx), side) / views
    return estimate


def solution(mesh):
    placed = (
        P(("gy", "gx"), None, None),
        P(("gy", "gx"), None),
        P(("gy", "gx")),
        P(),
        P(None, "gy", "gx"),
    )
    return jax.shard_map(
        local, mesh=mesh, in_specs=placed, out_specs=P(None, "gy", "gx"), check_vma=False
    )
```

time: 596 us -> 451 us (0.76)
  Pallas kernels: 0 us -> 113 us
  local copies, waits for them, and re-layouts: 153 us -> 41 us
  matrix products: 103 us -> 0 us
  waiting for transfers between devices: 199 us -> 161 us
  other arithmetic: 51.6 us -> 34.5 us
  starting transfers between devices: 81.4 us -> 96.5 us
    pallas_call x0 -> x9, Pallas kernels: none -> 113 us  [the longest x2 25.2 us: sides(): pl.pallas_call(sides_kernel, out_shape=jax.ShapeDtypeStruct((views, plane...]
    dot_general x14 -> x0, matrix products: 103 us -> none  [the longest x2 33.5 us: local(): jnp.einsum('vzjx,vxi->vzji', back_y, flip_x, preferred_element_type=jnp.f...]
    ppermute x8 -> x4, local copies, waits for them, and re-layouts: 66.9 us -> 5.96 us  [shift(): lax.ppermute(values, axis, pairs if way > 0 else [(b, a) for a, b in pairs])]
    slice x20, local copies, waits for them, and re-layouts: 71.2 us -> 19.7 us  [the longest x6 6.92 us: gathered(): lax.slice_in_dim(total, side + PAD, ext, axis=dim).astype(jnp.bfloat16)]
    concatenate x6, other arithmetic: 47.5 us -> 10.4 us  [the longest x4 7.13 us: widened(): jnp.concatenate([cells, shift(tail, axis, 1), shift(head, axis, -1)], axi...]
    ppermute x16, waiting for transfers between devices: 179 us -> 160 us  [shift(): lax.ppermute(values, axis, pairs if way > 0 else [(b, a) for a, b in pairs])]
    all_to_all x2, waiting for transfers between devices: 19.4 us -> 1.14 us  [the longest x1 1.14 us: local(): got_labels = exchange(labels.reshape(devices, slot_count)).reshape(-1)]
    ppermute x16, starting transfers between devices: 68.4 us -> 84.7 us  [shift(): lax.ppermute(values, axis, pairs if way > 0 else [(b, a) for a, b in pairs])]
  transfers between devices with their start and end apart: 18 -> 18, of which waited for: 15 -> 10; matrix products, arithmetic and copies ran while one was open for 16% -> 6% of each run, Pallas kernels for 0% -> 9%
where the time goes in v1:
time: 451 us; the launch traced here: 447 us
  waiting for transfers between devices  161 us (36%)
  Pallas kernels  113 us (25%)
  starting transfers between devices  96.5 us (21%)
  local copies, waits for them, and re-layouts  41 us (9%)
  other arithmetic  34.5 us (8%)
    ppermute x16, waiting for transfers between devices, shift(): lax.ppermute(values, axis, pairs if way > 0 else [(b, a) for a, b in pairs])  160 us
    ppermute x16, starting transfers between devices, shift(): lax.ppermute(values, axis, pairs if way > 0 else [(b, a) for a, b in pairs])  84.7 us
    pallas_call x2, Pallas kernels, sides(): pl.pallas_call(sides_kernel, out_shape=jax.ShapeDtypeStruct((views, plane...  25.2 us
    pallas_call x2, Pallas kernels, depth(): pl.pallas_call(depth_kernel, out_shape=jax.ShapeDtypeStruct(along.shape,...  24.3 us
    pallas_call x1, Pallas kernels, bands(): pl.pallas_call(functools.partial(bands_kernel, (taps.shape[1] - 1) // 2,...  23.2 us
    pallas_call x2, Pallas kernels, spread(): pl.pallas_call(spread_kernel, out_shape=jax.ShapeDtypeStruct((planes, ext...  21.8 us
    pallas_call x1, Pallas kernels, observe(): pl.pallas_call(functools.partial(observe_kernel, chunk), out_shape=jax.Sh...  13.5 us
    add x4, other arithmetic, gathered(): lax.slice_in_dim(inner, 0, PAD, axis=dim) + to_head  9.17 us
  transfers between devices with their start and end apart: 18, of which 10 were waited for; matrix products, arithmetic and copies ran while one was open for 6% of the time, Pallas kernels for 9%

profile of v1, /device:TPU:1, one launch (start us, length us, event | category | flops | bytes accessed | tf_op | source)
XLA Modules:
  0.0 447.4 jit_solution(9263546360193199434)
XLA Ops:
  3.0 7.1 %all-to-all-start = ((s32[32,1,8]{2,1,0:T(1,128)}), s32[32,1,8]{2,1,0:T(1,128)S(1)}, u32[]{:S(2)}, u32[]{:S(2)}) async-start(s32[32,1,8]{2,1,0:T(1,128)} %bitcast.1), calls=%async_computation | async-start | bytes 32768 | tf_op jit(solution)/shard_map/all_to_all | solution.py:305
  10.1 5.5 %pack.1 = bf16[256,128,128]{2,1,0:T(8,128)(2,1)} custom-call(s32[256]{0:T(256)} %get-tuple-element.17.pick_ref, bf16[128,128,128]{2,1,0:T(8,128)(2,1)} %tiles_ref.1), custom_call_target="tpu_custom_call" | custom-call | tf_op jit(solution)/shard_map/pack/pallas_call | solution.py:98
  16.8 4.8 %all-to-all-start.1 = ((bf16[32,8,128,128]{3,2,1,0:T(8,128)(2,1)}), bf16[32,8,128,128]{3,2,1,0:T(8,128)(2,1)}, u32[]{:S(2)}, u32[]{:S(2)}) async-start(bf16[32,8,128,128]{3,2,1,0:T(8,128)(2,1)} %bitcast.9), calls=%async_computation.1 | async-start | bytes 16777216 | tf_op jit(solution)/shard_map/all_to_all | solution.py:306
  21.8 3.3 collective-permute-start
  26.4 135.0 %collective-permute-done = bf16[32,16,128]{2,1,0:T(8,128)(2,1)S(1)} collective-permute-done((bf16[32,16,128]{2,1,0:T(8,128)(2,1)S(1)}, bf16[32,16,128]{2,1,0:T(8,128)(2,1)S(1)}, u32[]{:S(2)}, u32[]{:S(2)}) %collective-permute-start) | collective-permute-done | bytes 131104 | tf_op jit(solution)/shard_map/ppermute | solution.py:253
  164.9 3.3 collective-permute-start.2
  171.4 23.2 %bands.1 = (bf16[160,768]{1,0:T(8,128)(2,1)}, bf16[6,128,160]{2,1,0:T(8,128)(2,1)}, bf16[6,256,256]{2,1,0:T(8,128)(2,1)}, bf16[6,256,256]{2,1,0:T(8,128)(2,1)}, ...) custom-call(f32[18,31]{1,0:T(8,128)} %reshape.56.taps_ref), custom_call_target="tpu_custom_call" | custom-call | tf_op jit(solution)/shard_map/bands/pallas_call | solution.py:75
  199.2 3.5 pad_maximum_fusion.2.wide_ref
  202.6 12.6 %sides.2.sides_ref = bf16[6,32,128,128]{3,2,1,0:T(8,128)(2,1)} custom-call(bf16[32,160,160]{2,1,0:T(8,128)(2,1)} %pad_maximum_fusion.2.wide_ref, bf16[160,768]{1,0:T(8,128)(2,1)} %get-tuple-element.11.bx_ref, bf16[6,128,160]{2,1,0:T(8,128)(2,1)} %get-tuple-element.12.by_ref), custom_call_target="tpu_custom_call" | custom-call | flops 2264924160 | bytes 9437184 | tf_op jit(solution)/shard_map/sides/pallas_call | solution.py:164
  215.2 13.5 %observe.1 = f32[192,128,128]{2,1,0:T(8,128)} custom-call(s32[256]{0:T(256)} %copy-done.11, bf16[256,128,128]{2,1,0:T(8,128)(2,1)} %bitcast.3.tiles_ref), custom_call_target="tpu_custom_call" | custom-call | tf_op jit(solution)/shard_map/observe/pallas_call | solution.py:135
  229.5 12.1 %depth.2.back_ref = bf16[6,32,128,128]{3,2,1,0:T(8,128)(2,1)} custom-call(bf16[6,32,128,128]{3,2,1,0:T(8,128)(2,1)} %sides.2.sides_ref, f32[6,32,128,128]{3,2,1,0:T(8,128)} %bitcast.7, f32[6,32,128]{2,1,0:T(8,128)} %broadcast_in_dim.37.count_ref, bf16[6,256,256]{2,1,0:T(8,128)(2,1)} %get-tuple-element.13.kz_ref, bf16[6,256,256]{2,1,0:T(8,128)(2,1)} %get-tuple-element.14.kf_ref), custom_call_target="tpu_custom_call" | custom-call | tf_op jit(solution)/shard_map/depth/pallas_call | solution.py:207
  241.6 10.9 %spread.2 = f32[32,160,256]{2,1,0:T(8,128)} custom-call(bf16[6,32,128,128]{3,2,1,0:T(8,128)(2,1)} %depth.2.back_ref, bf16[6,160,128]{2,1,0:T(8,128)(2,1)} %get-tuple-element.15.fy_ref, bf16[768,256]{1,0:T(8,128)(2,1)} %get-tuple-element.16.fx_ref), custom_call_target="tpu_custom_call" | custom-call | tf_op jit(solution)/shard_map/spread/pallas_call | solution.py:235
  252.5 3.0 convert.17
  255.5 49.9 %collective-permute-start.4 = (bf16[32,16,256]{2,1,0:T(8,128)(2,1)S(1)}, bf16[32,16,256]{2,1,0:T(8,128)(2,1)S(1)}, u32[]{:S(2)}, u32[]{:S(2)}) collective-permute-start(bf16[32,16,256]{2,1,0:T(8,128)(2,1)S(1)} %get-tuple-element.31), channel_id=1, source_target_pairs={{0,8},{8,16},{16,24},{1,9},{9,17},{17,25},{2,10},{10,18},{18,26},{... | collective-permute-start | bytes 786440 | tf_op jit(solution)/shard_map/ppermute | solution.py:253
  307.0 4.5 collective-permute-done.4
  311.4 4.1 collective-permute-done.5
  331.5 2.6 copy.31
  334.1 4.4 slice_add_fusion.3
  338.5 2.5 fusion.9
  345.9 4.1 collective-permute-done.9
  353.6 4.7 %collective-permute-start.10 = (bf16[32,160,16]{1,2,0:T(8,128)(2,1)S(1)}, bf16[32,160,16]{1,2,0:T(8,128)(2,1)S(1)}, u32[]{:S(2)}, u32[]{:S(2)}) collective-permute-start(bf16[32,160,16]{1,2,0:T(8,128)(2,1)S(1)} %copy.32), channel_id=1, source_target_pairs={{0,1},{1,2},{2,3},{3,4},{4,5},{5,6},{6,7},{8,9},{9,10},{10,11},{11... | collective-permute-start | bytes 491528 | tf_op jit(solution)/shard_map/ppermute | solution.py:253
  362.1 4.9 %collective-permute-done.11 = bf16[32,160,16]{1,2,0:T(8,128)(2,1)} collective-permute-done((bf16[32,160,16]{1,2,0:T(8,128)(2,1)S(1)}, bf16[32,160,16]{1,2,0:T(8,128)(2,1)}, u32[]{:S(2)}, u32[]{:S(2)}) %collective-permute-start.11) | collective-permute-done | bytes 163872 | tf_op jit(solution)/shard_map/ppermute | solution.py:253
  369.4 3.5 pad_maximum_fusion.3.wide_ref
  372.9 12.6 %sides.3.sides_ref = bf16[6,32,128,128]{3,2,1,0:T(8,128)(2,1)} custom-call(bf16[32,160,160]{2,1,0:T(8,128)(2,1)} %pad_maximum_fusion.3.wide_ref, bf16[160,768]{1,0:T(8,128)(2,1)} %get-tuple-element.11.bx_ref, bf16[6,128,160]{2,1,0:T(8,128)(2,1)} %get-tuple-element.12.by_ref), custom_call_target="tpu_custom_call" | custom-call | flops 2264924160 | bytes 9437184 | tf_op jit(solution)/shard_map/sides/pallas_call | solution.py:164
  385.5 12.1 %depth.3.back_ref = bf16[6,32,128,128]{3,2,1,0:T(8,128)(2,1)} custom-call(bf16[6,32,128,128]{3,2,1,0:T(8,128)(2,1)} %sides.3.sides_ref, f32[6,32,128,128]{3,2,1,0:T(8,128)} %bitcast.8, f32[6,32,128]{2,1,0:T(8,128)} %broadcast_in_dim.37.count_ref, bf16[6,256,256]{2,1,0:T(8,128)(2,1)} %get-tuple-element.13.kz_ref, bf16[6,256,256]{2,1,0:T(8,128)(2,1)} %get-tuple-element.14.kf_ref), custom_call_target="tpu_custom_call" | custom-call | tf_op jit(solution)/shard_map/depth/pallas_call | solution.py:207
  397.6 10.9 %spread.3 = f32[32,160,256]{2,1,0:T(8,128)} custom-call(bf16[6,32,128,128]{3,2,1,0:T(8,128)(2,1)} %depth.3.back_ref, bf16[6,160,128]{2,1,0:T(8,128)(2,1)} %get-tuple-element.15.fy_ref, bf16[768,256]{1,0:T(8,128)(2,1)} %get-tuple-element.16.fx_ref), custom_call_target="tpu_custom_call" | custom-call | tf_op jit(solution)/shard_map/spread/pallas_call | solution.py:235
  408.5 3.0 convert.19
  416.6 3.8 collective-permute-done.13
  425.0 3.8 collective-permute-start.14
  437.9 2.6 copy.39
  440.5 4.4 slice_add_fusion.1
  444.9 2.5 fusion.2
  (97 shorter events, 68.2 us)
Async XLA Ops:
  3.0 13.8 %all-to-all-start = ((s32[32,1,8]{2,1,0:T(1,128)}), s32[32,1,8]{2,1,0:T(1,128)S(1)}, u32[]{:S(2)}, u32[]{:S(2)}) async-start(s32[32,1,8]{2,1,0:T(1,128)} %bitcast.1), calls=%async_computation | async-start | bytes 32768 | tf_op jit(solution)/shard_map/all_to_all | solution.py:305
  16.8 4.8 %copy-start.5 = (f32[32,128,128]{2,1,0:T(8,128)S(1)}, f32[32,128,128]{2,1,0:T(8,128)}, u32[]{:S(2)}) copy-start(f32[32,128,128]{2,1,0:T(8,128)} %param.9) | copy-start | bytes 6291460
  16.8 198.4 %all-to-all-start.1 = ((bf16[32,8,128,128]{3,2,1,0:T(8,128)(2,1)}), bf16[32,8,128,128]{3,2,1,0:T(8,128)(2,1)}, u32[]{:S(2)}, u32[]{:S(2)}) async-start(bf16[32,8,128,128]{3,2,1,0:T(8,128)(2,1)} %bitcast.9), calls=%async_computation.1 | async-start | bytes 16777216 | tf_op jit(solution)/shard_map/all_to_all | solution.py:306
  21.8 139.6 %collective-permute-start = (bf16[32,16,128]{2,1,0:T(8,128)(2,1)S(1)}, bf16[32,16,128]{2,1,0:T(8,128)(2,1)S(1)}, u32[]{:S(2)}, u32[]{:S(2)}) collective-permute-start(bf16[32,16,128]{2,1,0:T(8,128)(2,1)S(1)} %get-tuple-element.43), channel_id=1, source_target_pairs={{0,8},{8,16},{16,24},{1,9},{9,17},{17,25},{2,10},{10,18},{18,26},{... | collective-permute-start | bytes 393224 | tf_op jit(solution)/shard_map/ppermute | solution.py:253
  25.1 136.3 %collective-permute-start.1 = (bf16[32,16,128]{2,1,0:T(8,128)(2,1)S(1)}, bf16[32,16,128]{2,1,0:T(8,128)(2,1)S(1)}, u32[]{:S(2)}, u32[]{:S(2)}) collective-permute-start(bf16[32,16,128]{2,1,0:T(8,128)(2,1)S(1)} %get-tuple-element.44), channel_id=1, source_target_pairs={{8,0},{16,8},{24,16},{9,1},{17,9},{25,17},{10,2},{18,10},{26,18},{... | collective-permute-start | bytes 393224 | tf_op jit(solution)/shard_map/ppermute | solution.py:253
  163.0 7.7 %copy-start.12 = (f32[6,3,31]{2,1,0:T(4,128)S(1)}, f32[6,3,31]{2,1,0:T(4,128)}, u32[]{:S(2)}) copy-start(f32[6,3,31]{2,1,0:T(4,128)} %param.8) | copy-start | bytes 6700
  164.9 31.2 %collective-permute-start.2 = (bf16[32,160,16]{1,2,0:T(8,128)(2,1)S(1)}, bf16[32,160,16]{1,2,0:T(8,128)(2,1)S(1)}, u32[]{:S(2)}, u32[]{:S(2)}) collective-permute-start(bf16[32,160,16]{1,2,0:T(8,128)(2,1)S(1)} %copy.23), channel_id=1, source_target_pairs={{0,1},{1,2},{2,3},{3,4},{4,5},{5,6},{6,7},{8,9},{9,10},{10,11},{11... | collective-permute-start | bytes 491528 | tf_op jit(solution)/shard_map/ppermute | solution.py:253
  168.8 27.9 %collective-permute-start.3 = (bf16[32,160,16]{1,2,0:T(8,128)(2,1)S(1)}, bf16[32,160,16]{1,2,0:T(8,128)(2,1)}, u32[]{:S(2)}, u32[]{:S(2)}) collective-permute-start(bf16[32,160,16]{1,2,0:T(8,128)(2,1)S(1)} %copy.24), channel_id=1, source_target_pairs={{1,0},{2,1},{3,2},{4,3},{5,4},{6,5},{7,6},{9,8},{10,9},{11,10},{12... | collective-permute-start | bytes 491528 | tf_op jit(solution)/shard_map/ppermute | solution.py:253
  195.9 6.7 %copy-start.11 = (s32[256]{0:T(256)}, s32[256]{0:T(256)S(1)}, u32[]{:S(2)}) copy-start(s32[256]{0:T(256)S(1)} %reshape.51.label_ref) | copy-start | bytes 3076
  252.5 54.3 %copy-start.1 = (f32[32,160,256]{2,1,0:T(8,128)S(1)}, f32[32,160,256]{2,1,0:T(8,128)}, u32[]{:S(2)}) copy-start(f32[32,160,256]{2,1,0:T(8,128)} %spread.2) | copy-start | bytes 15728644
  255.5 55.9 %collective-permute-start.4 = (bf16[32,16,256]{2,1,0:T(8,128)(2,1)S(1)}, bf16[32,16,256]{2,1,0:T(8,128)(2,1)S(1)}, u32[]{:S(2)}, u32[]{:S(2)}) collective-permute-start(bf16[32,16,256]{2,1,0:T(8,128)(2,1)S(1)} %get-tuple-element.31), channel_id=1, source_target_pairs={{0,8},{8,16},{16,24},{1,9},{9,17},{17,25},{2,10},{10,18},{18,26},{... | collective-permute-start | bytes 786440 | tf_op jit(solution)/shard_map/ppermute | solution.py:253
  305.5 10.1 %collective-permute-start.5 = (bf16[32,16,256]{2,1,0:T(8,128)(2,1)S(1)}, bf16[32,16,256]{2,1,0:T(8,128)(2,1)S(1)}, u32[]{:S(2)}, u32[]{:S(2)}) collective-permute-start(bf16[32,16,256]{2,1,0:T(8,128)(2,1)S(1)} %get-tuple-element.32), channel_id=1, source_target_pairs={{8,0},{16,8},{24,16},{9,1},{17,9},{25,17},{10,2},{18,10},{26,18},{... | collective-permute-start | bytes 786440 | tf_op jit(solution)/shard_map/ppermute | solution.py:253
  315.7 0.8 copy-start.7
  315.7 1.0 copy-start.8
  320.1 9.7 %collective-permute-start.6 = (bf16[32,128,16]{1,2,0:T(8,128)(2,1)S(1)}, bf16[32,128,16]{1,2,0:T(8,128)(2,1)S(1)}, u32[]{:S(2)}, u32[]{:S(2)}) collective-permute-start(bf16[32,128,16]{1,2,0:T(8,128)(2,1)S(1)} %copy.28), channel_id=1, source_target_pairs={{0,1},{1,2},{2,3},{3,4},{4,5},{5,6},{6,7},{8,9},{9,10},{10,11},{11... | collective-permute-start | bytes 393224 | tf_op jit(solution)/shard_map/ppermute | solution.py:253
  324.1 7.4 %collective-permute-start.7 = (bf16[32,128,16]{1,2,0:T(8,128)(2,1)S(1)}, bf16[32,128,16]{1,2,0:T(8,128)(2,1)}, u32[]{:S(2)}, u32[]{:S(2)}) collective-permute-start(bf16[32,128,16]{1,2,0:T(8,128)(2,1)S(1)} %copy.30), channel_id=1, source_target_pairs={{1,0},{2,1},{3,2},{4,3},{5,4},{6,5},{7,6},{9,8},{10,9},{11,10},{12... | collective-permute-start | bytes 393224 | tf_op jit(solution)/shard_map/ppermute | solution.py:253
  327.9 2.0 copy-start.2
  334.1 4.4 copy-start.6
  341.1 4.9 %collective-permute-start.8 = (bf16[32,16,128]{2,1,0:T(8,128)(2,1)S(1)}, bf16[32,16,128]{2,1,0:T(8,128)(2,1)S(1)}, u32[]{:S(2)}, u32[]{:S(2)}) collective-permute-start(bf16[32,16,128]{2,1,0:T(8,128)(2,1)S(1)} %get-tuple-element.41), channel_id=1, source_target_pairs={{0,8},{8,16},{16,24},{1,9},{9,17},{17,25},{2,10},{10,18},{18,26},{... | collective-permute-start | bytes 393224 | tf_op jit(solution)/shard_map/ppermute | solution.py:253
  343.3 6.8 %collective-permute-start.9 = (bf16[32,16,128]{2,1,0:T(8,128)(2,1)S(1)}, bf16[32,16,128]{2,1,0:T(8,128)(2,1)S(1)}, u32[]{:S(2)}, u32[]{:S(2)}) collective-permute-start(bf16[32,16,128]{2,1,0:T(8,128)(2,1)S(1)} %get-tuple-element.42), channel_id=1, source_target_pairs={{8,0},{16,8},{24,16},{9,1},{17,9},{25,17},{10,2},{18,10},{26,18},{... | collective-permute-start | bytes 393224 | tf_op jit(solution)/shard_map/ppermute | solution.py:253
  353.6 8.0 %collective-permute-start.10 = (bf16[32,160,16]{1,2,0:T(8,128)(2,1)S(1)}, bf16[32,160,16]{1,2,0:T(8,128)(2,1)S(1)}, u32[]{:S(2)}, u32[]{:S(2)}) collective-permute-start(bf16[32,160,16]{1,2,0:T(8,128)(2,1)S(1)} %copy.32), channel_id=1, source_target_pairs={{0,1},{1,2},{2,3},{3,4},{4,5},{5,6},{6,7},{8,9},{9,10},{10,11},{11... | collective-permute-start | bytes 491528 | tf_op jit(solution)/shard_map/ppermute | solution.py:253
  358.9 8.1 %collective-permute-start.11 = (bf16[32,160,16]{1,2,0:T(8,128)(2,1)S(1)}, bf16[32,160,16]{1,2,0:T(8,128)(2,1)}, u32[]{:S(2)}, u32[]{:S(2)}) collective-permute-start(bf16[32,160,16]{1,2,0:T(8,128)(2,1)S(1)} %copy.33), channel_id=1, source_target_pairs={{1,0},{2,1},{3,2},{4,3},{5,4},{6,5},{7,6},{9,8},{10,9},{11,10},{12... | collective-permute-start | bytes 491528 | tf_op jit(solution)/shard_map/ppermute | solution.py:253
  408.5 6.1 %copy-start = (f32[32,160,256]{2,1,0:T(8,128)S(1)}, f32[32,160,256]{2,1,0:T(8,128)}, u32[]{:S(2)}) copy-start(f32[32,160,256]{2,1,0:T(8,128)} %spread.3) | copy-start | bytes 15728644
  411.6 5.0 %collective-permute-start.12 = (bf16[32,16,256]{2,1,0:T(8,128)(2,1)S(1)}, bf16[32,16,256]{2,1,0:T(8,128)(2,1)S(1)}, u32[]{:S(2)}, u32[]{:S(2)}) collective-permute-start(bf16[32,16,256]{2,1,0:T(8,128)(2,1)S(1)} %get-tuple-element.29), channel_id=1, source_target_pairs={{0,8},{8,16},{16,24},{1,9},{9,17},{17,25},{2,10},{10,18},{18,26},{... | collective-permute-start | bytes 786440 | tf_op jit(solution)/shard_map/ppermute | solution.py:253
  413.3 7.1 %collective-permute-start.13 = (bf16[32,16,256]{2,1,0:T(8,128)(2,1)S(1)}, bf16[32,16,256]{2,1,0:T(8,128)(2,1)S(1)}, u32[]{:S(2)}, u32[]{:S(2)}) collective-permute-start(bf16[32,16,256]{2,1,0:T(8,128)(2,1)S(1)} %get-tuple-element.30), channel_id=1, source_target_pairs={{8,0},{16,8},{24,16},{9,1},{17,9},{25,17},{10,2},{18,10},{26,18},{... | collective-permute-start | bytes 786440 | tf_op jit(solution)/shard_map/ppermute | solution.py:253
  420.6 0.8 copy-start.9
  420.6 1.0 copy-start.10
  425.0 11.2 %collective-permute-start.14 = (bf16[32,128,16]{1,2,0:T(8,128)(2,1)S(1)}, bf16[32,128,16]{1,2,0:T(8,128)(2,1)S(1)}, u32[]{:S(2)}, u32[]{:S(2)}) collective-permute-start(bf16[32,128,16]{1,2,0:T(8,128)(2,1)S(1)} %copy.36), channel_id=1, source_target_pairs={{0,1},{1,2},{2,3},{3,4},{4,5},{5,6},{6,7},{8,9},{9,10},{10,11},{11... | collective-permute-start | bytes 393224 | tf_op jit(solution)/shard_map/ppermute | solution.py:253
  430.4 7.5 %collective-permute-start.15 = (bf16[32,128,16]{1,2,0:T(8,128)(2,1)S(1)}, bf16[32,128,16]{1,2,0:T(8,128)(2,1)}, u32[]{:S(2)}, u32[]{:S(2)}) collective-permute-start(bf16[32,128,16]{1,2,0:T(8,128)(2,1)S(1)} %copy.38), channel_id=1, source_target_pairs={{1,0},{2,1},{3,2},{4,3},{5,4},{6,5},{7,6},{9,8},{10,9},{11,10},{12... | collective-permute-start | bytes 393224 | tf_op jit(solution)/shard_map/ppermute | solution.py:253
  434.2 2.0 copy-start.3
  440.5 4.4 copy-start.4

commit v2 on v1

--- a/solution.py
+++ b/solution.py
@@ -57,7 +57,8 @@
         by_ref[v] = long_y[:, :ext].astype(jnp.bfloat16)
         tall_x = toeplitz(taps_ref, 3 * v + 2, tall_off)
         long_x = toeplitz(taps_ref, 3 * v + 2, long_off)
-        bx_ref[:, v * side : (v + 1) * side] = tall_x.astype(jnp.bfloat16)
+        bx_ref[:ext, v * side : (v + 1) * side] = tall_x.astype(jnp.bfloat16)
+        bx_ref[ext:, v * side : (v + 1) * side] = jnp.zeros((wide - ext, side), jnp.bfloat16)
         fx_ref[v * side : (v + 1) * side, :] = long_x.astype(jnp.bfloat16)
 
 
@@ -65,7 +66,7 @@
     views = taps.shape[0] // 3
     ext = side + 2 * PAD
     shapes = [
-        (ext, views * side),
+        (2 * side, views * side),
         (views, side, ext),
         (views, planes * 8, planes * 8),
         (views, planes * 8, planes * 8),
@@ -166,7 +167,7 @@
         out_shape=jax.ShapeDtypeStruct((views, planes, side, side), jnp.bfloat16),
         grid=(planes // chunk,),
         in_specs=[
-            pl.BlockSpec((chunk, ext, ext), lambda i: (i, 0, 0)),
+            pl.BlockSpec((chunk,) + wide.shape[1:], lambda i: (i, 0, 0)),
             pl.BlockSpec(bx.shape, lambda i: (0, 0)),
             pl.BlockSpec(by.shape, lambda i: (0, 0, 0)),
         ],
@@ -215,8 +216,22 @@
     )(along, seen, count, kz, kf)
 
 
-def spread_kernel(back_ref, fy_ref, fx_ref, out_ref):
-    views, planes, _, _ = back_ref.shape
+def fold_lanes(values, start):
+    lane = lax.broadcasted_iota(jnp.int32, values[0].shape, 1)
+    held = jnp.zeros(values[0].shape, jnp.float32)
+    for k, one in enumerate(values):
+        held = jnp.where(lane // PAD == k, pltpu.roll(one, (PAD * k - start) % 128, 1), held)
+    return held
+
+
+def unfold_lanes(held, k, start):
+    lane = lax.broadcasted_iota(jnp.int32, held.shape, 1)
+    return jnp.where(lane // PAD == start // PAD, pltpu.roll(held, (start - PAD * k) % 128, 1), 0.0)
+
+
+def spread_kernel(back_ref, fy_ref, fx_ref, in_ref, ys_ref, xl_ref, xr_ref):
+    views, planes, side, _ = back_ref.shape
+    rims = []
     for z in range(planes):
         wide = jnp.concatenate(
             [
@@ -225,62 +240,240 @@
             ],
             axis=1,
         )
-        out_ref[z] = jnp.dot(wide, fx_ref[...], preferred_element_type=jnp.float32)
+        part = jnp.dot(wide, fx_ref[...], preferred_element_type=jnp.float32)
+        in_ref[z] = part[:side, :side]
+        ys_ref[z] = part[side:, :side].astype(jnp.bfloat16)
+        rims.append(part[:, side:])
+    xl_ref[0] = fold_lanes(rims, 0).astype(jnp.bfloat16)
+    xr_ref[0] = fold_lanes(rims, PAD).astype(jnp.bfloat16)
 
 
 def spread(back, fy, fx):
     views, planes, side, _ = back.shape
     ext = fy.shape[1]
-    chunk = 4
+    chunk = 8
+    folds = planes // chunk
+    fold = pl.BlockSpec((1, ext, side), lambda i: (i, 0, 0))
     return pl.pallas_call(
         spread_kernel,
-        out_shape=jax.ShapeDtypeStruct((planes, ext, fx.shape[1]), jnp.float32),
-        grid=(planes // chunk,),
+        out_shape=[
+            jax.ShapeDtypeStruct((planes, side, side), jnp.float32),
+            jax.ShapeDtypeStruct((planes, 2 * PAD, side), jnp.bfloat16),
+            jax.ShapeDtypeStruct((folds, ext, side), jnp.bfloat16),
+            jax.ShapeDtypeStruct((folds, ext, side), jnp.bfloat16),
+        ],
+        grid=(folds,),
         in_specs=[
             pl.BlockSpec((views, chunk, side, side), lambda i: (0, i, 0, 0)),
             pl.BlockSpec(fy.shape, lambda i: (0, 0, 0)),
             pl.BlockSpec(fx.shape, lambda i: (0, 0)),
         ],
-        out_specs=pl.BlockSpec((chunk, ext, fx.shape[1]), lambda i: (i, 0, 0)),
+        out_specs=[
+            pl.BlockSpec((chunk, side, side), lambda i: (i, 0, 0)),
+            pl.BlockSpec((chunk, 2 * PAD, side), lambda i: (i, 0, 0)),
+            fold,
+            fold,
+        ],
         compiler_params=pltpu.CompilerParams(vmem_limit_bytes=VMEM),
         name="spread",
     )(back, fy, fx)
 
 
-def shift(values, axis, way):
-    count = lax.axis_size(axis)
-    pairs = [(i, i + 1) for i in range(count - 1)]
-    return lax.ppermute(values, axis, pairs if way > 0 else [(b, a) for a, b in pairs])
-
-
-def widened(estimate):
-    cells = estimate.astype(jnp.bfloat16)
-    for axis, dim in (("gy", 1), ("gx", 2)):
-        side = cells.shape[dim]
-        head = lax.slice_in_dim(cells, 0, PAD, axis=dim)
-        tail = lax.slice_in_dim(cells, side - PAD, side, axis=dim)
-        cells = jnp.concatenate([cells, shift(tail, axis, 1), shift(head, axis, -1)], axis=dim)
-    return cells
-
-
-def gathered(partial, side):
+NEAR = [(-1, 0), (1, 0), (0, -1), (0, 1), (-1, -1), (1, -1), (-1, 1), (1, 1)]
+
+
+def inside(grid, dy, dx):
+    ny, nx = grid
+    y = lax.axis_index("gy") + dy
+    x = lax.axis_index("gx") + dx
+    return (y >= 0) & (y < ny) & (x >= 0) & (x < nx), (y, x)
+
+
+def greet(grid):
+    barrier = pltpu.get_barrier_semaphore()
+    for dy, dx in NEAR:
+        there, where = inside(grid, dy, dx)
+
+        @pl.when(there)
+        def _():
+            pl.semaphore_signal(barrier, inc=1, device_id=where, device_id_type=pl.DeviceIdType.MESH)
+
+    ny, nx = grid
+    y, x = lax.axis_index("gy"), lax.axis_index("gx")
+    tall = 3 - (y == 0).astype(jnp.int32) - (y == ny - 1).astype(jnp.int32)
+    broad = 3 - (x == 0).astype(jnp.int32) - (x == nx - 1).astype(jnp.int32)
+    pl.semaphore_wait(barrier, tall * broad - 1)
+
+
+def swap(grid, moves, send_sems, recv_sems):
+    def copy(i, where):
+        source, dest = moves[i]
+        return pltpu.make_async_remote_copy(
+            src_ref=source, dst_ref=dest, send_sem=send_sems.at[i], recv_sem=recv_sems.at[i],
+            device_id=where, device_id_type=pl.DeviceIdType.MESH,
+        )
+
+    for i, (dy, dx) in enumerate(NEAR):
+        there, where = inside(grid, dy, dx)
+
+        @pl.when(there)
+        def _():
+            copy(i, where).start()
+
+    for i, (dy, dx) in enumerate(NEAR):
+        there, where = inside(grid, -dy, -dx)
+
+        @pl.when(there)
+        def _():
+            copy(i, where).wait_recv()
+
+        @pl.when(jnp.logical_not(there))
+        def _():
+            dest = moves[i][1]
+            dest[...] = jnp.zeros(dest.shape, dest.dtype)
+
+    for i, (dy, dx) in enumerate(NEAR):
+        there, where = inside(grid, dy, dx)
+
+        @pl.when(there)
+        def _():
+            copy(i, where).wait_send()
+
+
+def widen(grid, fresh, wide_ref, left, right, rows, from_left, from_right, send_sems, recv_sems):
+    planes, ext, _ = wide_ref.shape
+    side = ext - 2 * PAD
+
+    def cut(p, carry):
+        values = []
+        for k in range(8):
+            plane = fresh(p * 8 + k)
+            values.append(plane)
+            wide_ref[p * 8 + k, :side, :side] = plane.astype(jnp.bfloat16)
+        left[p] = fold_lanes(values, 0).astype(jnp.bfloat16)
+        right[p] = fold_lanes(values, side - PAD).astype(jnp.bfloat16)
+        return carry
+
+    lax.fori_loop(0, planes // 8, cut, 0)
+    first, last = pl.ds(0, PAD), pl.ds(side - PAD, PAD)
+    whole, before, after = pl.ds(0, side), pl.ds(side, PAD), pl.ds(side + PAD, PAD)
+    lanes = pl.ds(0, side)
+    moves = [
+        (wide_ref.at[:, first, lanes], rows.at[:, pl.ds(PAD, PAD)]),
+        (wide_ref.at[:, last, lanes], rows.at[:, pl.ds(0, PAD)]),
+        (left, from_right.at[:, whole]),
+        (right, from_left.at[:, whole]),
+        (left.at[:, first], from_right.at[:, after]),
+        (left.at[:, last], from_right.at[:, before]),
+        (right.at[:, first], from_left.at[:, after]),
+        (right.at[:, last], from_left.at[:, before]),
+    ]
+    swap(grid, moves, send_sems, recv_sems)
+
+    def paste(p, carry):
+        low = from_left[p].astype(jnp.float32)
+        high = from_right[p].astype(jnp.float32)
+        for k in range(8):
+            rim = unfold_lanes(low, k, 0) + unfold_lanes(high, k, PAD)
+            wide_ref[p * 8 + k, :, side:] = rim.astype(jnp.bfloat16)
+            wide_ref[p * 8 + k, side:, :side] = rows[p * 8 + k]
+        return carry
+
+    lax.fori_loop(0, planes // 8, paste, 0)
+
+
+def rim_scratch(planes, side):
     ext = side + 2 * PAD
-    total = partial
-    for axis, dim in (("gy", 1), ("gx", 2)):
-        before = lax.slice_in_dim(total, side, side + PAD, axis=dim).astype(jnp.bfloat16)
-        after = lax.slice_in_dim(total, side + PAD, ext, axis=dim).astype(jnp.bfloat16)
-        to_tail = shift(before, axis, -1).astype(jnp.float32)
-        to_head = shift(after, axis, 1).astype(jnp.float32)
-        inner = lax.slice_in_dim(total, 0, side, axis=dim)
-        total = jnp.concatenate(
-            [
-                lax.slice_in_dim(inner, 0, PAD, axis=dim) + to_head,
-                lax.slice_in_dim(inner, PAD, side - PAD, axis=dim),
-                lax.slice_in_dim(inner, side - PAD, side, axis=dim) + to_tail,
-            ],
-            axis=dim,
-        )
-    return total
+    return [
+        pltpu.VMEM((planes, 2 * PAD, side), jnp.bfloat16),
+        pltpu.VMEM((planes // 8, ext, side), jnp.bfloat16),
+        pltpu.VMEM((planes // 8, ext, side), jnp.bfloat16),
+        pltpu.SemaphoreType.DMA((8,)),
+        pltpu.SemaphoreType.DMA((8,)),
+    ]
+
+
+def fold_scratch(planes, side):
+    return [pltpu.VMEM((planes // 8, side, side), jnp.bfloat16)] * 2
+
+
+def gather(grid, in_ref, ys_ref, xl_ref, xr_ref, rows, from_left, from_right, send_sems, recv_sems):
+    planes, side, _ = in_ref.shape
+    whole, before, after = pl.ds(0, side), pl.ds(side, PAD), pl.ds(side + PAD, PAD)
+    first, second = pl.ds(0, PAD), pl.ds(PAD, PAD)
+    moves = [
+        (ys_ref.at[:, first], rows.at[:, second]),
+        (ys_ref.at[:, second], rows.at[:, first]),
+        (xl_ref.at[:, whole], from_right.at[:, whole]),
+        (xr_ref.at[:, whole], from_left.at[:, whole]),
+        (xl_ref.at[:, before], from_right.at[:, after]),
+        (xl_ref.at[:, after], from_right.at[:, before]),
+        (xr_ref.at[:, before], from_left.at[:, after]),
+        (xr_ref.at[:, after], from_left.at[:, before]),
+    ]
+    swap(grid, moves, send_sems, recv_sems)
+
+
+def totals(z, p, k, in_ref, rows, from_left, from_right):
+    side = in_ref.shape[1]
+    gap = jnp.zeros((side - 2 * PAD, side), jnp.float32)
+    edge = rows[z].astype(jnp.float32)
+
+    def rim(held, start):
+        held = held.astype(jnp.float32)
+        body = held[:side] + jnp.concatenate([held[side : side + PAD], gap, held[side + PAD :]], axis=0)
+        return unfold_lanes(body, k, start)
+
+    total = in_ref[z] + jnp.concatenate([edge[:PAD], gap, edge[PAD:]], axis=0)
+    return total + rim(from_left[p], 0) + rim(from_right[p], side - PAD)
+
+
+def first_kernel(grid, est_ref, wide_ref, left, right, *rim):
+    greet(grid)
+    widen(grid, lambda z: est_ref[z], wide_ref, left, right, *rim)
+
+
+def between_kernel(grid, views, est_ref, in_ref, ys_ref, xl_ref, xr_ref, new_ref, wide_ref, *scratch):
+    greet(grid)
+    rim, (left, right), again = scratch[:5], scratch[5:7], scratch[7:]
+    gather(grid, in_ref, ys_ref, xl_ref, xr_ref, *rim)
+
+    def update(p, carry):
+        for k in range(8):
+            z = p * 8 + k
+            new_ref[z] = est_ref[z] * totals(z, p, k, in_ref, *rim[:3]) / views
+        return carry
+
+    lax.fori_loop(0, est_ref.shape[0] // 8, update, 0)
+    widen(grid, lambda z: new_ref[z], wide_ref, left, right, *again)
+
+
+def last_kernel(grid, in_ref, ys_ref, xl_ref, xr_ref, out_ref, *rim):
+    greet(grid)
+    gather(grid, in_ref, ys_ref, xl_ref, xr_ref, *rim)
+
+    def update(p, carry):
+        for k in range(8):
+            z = p * 8 + k
+            out_ref[z] = totals(z, p, k, in_ref, *rim[:3])
+        return carry
+
+    lax.fori_loop(0, in_ref.shape[0] // 8, update, 0)
+
+
+def rim_call(kernel, name, number, shapes, scratch, args):
+    held = pl.BlockSpec(memory_space=pltpu.VMEM)
+    return pl.pallas_call(
+        kernel,
+        out_shape=shapes,
+        in_specs=[held] * len(args),
+        out_specs=[held] * len(shapes),
+        scratch_shapes=scratch,
+        compiler_params=pltpu.CompilerParams(
+            vmem_limit_bytes=VMEM, collective_id=number, has_side_effects=True
+        ),
+        name=name,
+    )(*args)
 
 
 def local(tiles, tile_dest, tile_slot, psf, estimate):
@@ -303,21 +496,35 @@
         lax.all_to_all, axis_name=("gy", "gx"), split_axis=0, concat_axis=0, tiled=True
     )
     got_labels = exchange(labels.reshape(devices, slot_count)).reshape(-1)
+    grid = (lax.axis_size("gy"), lax.axis_size("gx"))
+    volume = jax.ShapeDtypeStruct(estimate.shape, jnp.float32)
+    framed = jax.ShapeDtypeStruct((planes, side + 2 * PAD, 2 * side), jnp.bfloat16)
+    rim, folds = rim_scratch(planes, side), fold_scratch(planes, side)
+    (wide,) = rim_call(functools.partial(first_kernel, grid), "rim_first", 0, [framed], folds + rim, [estimate])
+    packed, wide, got_labels = lax.optimization_barrier((packed, wide, got_labels))
     got_tiles = exchange(packed.reshape(devices, slot_count, side, side)).reshape(-1, side, side)
 
     kernel = (psf / jnp.sum(psf, axis=2, keepdims=True)).astype(jnp.bfloat16).astype(jnp.float32)
     bx, by, kz, kf, fy, fx = bands(kernel.reshape(views * 3, taps), planes, side)
-    along = sides(widened(estimate), bx, by)
-
-    seen = observe(got_labels, got_tiles, views * planes).reshape(views, planes, side, side)
+
     sorting = got_labels[None, :] == jnp.arange(views * planes)[:, None]
     counted = jnp.sum(sorting.astype(jnp.float32), axis=1).reshape(views, planes)
     count = jnp.broadcast_to(counted[:, :, None], (views, planes, side))
+    seen = None
     for repeat_index in range(ITERS):
-        if repeat_index:
-            along = sides(widened(estimate), bx, by)
+        along = sides(wide, bx, by)
+        if seen is None:
+            seen = observe(got_labels, got_tiles, views * planes).reshape(views, planes, side, side)
         back = depth(along, seen, count, kz, kf)
-        estimate = estimate * gathered(spread(back, fy, fx), side) / views
+        parts = spread(back, fy, fx)
+        if repeat_index + 1 < ITERS:
+            estimate, wide = rim_call(
+                functools.partial(between_kernel, grid, views), "rim_between", 1,
+                [volume, framed], rim + folds + rim, [estimate, *parts],
+            )
+        else:
+            (total,) = rim_call(functools.partial(last_kernel, grid), "rim_last", 2, [volume], rim, parts)
+            estimate = estimate * total / views
     return estimate
 
 

time: 451 us -> 323 us (0.72)
  starting transfers between devices: 96.5 us -> 12 us
  Pallas kernels: 113 us -> 152 us
  local copies, waits for them, and re-layouts: 41 us -> 2.72 us
  other arithmetic: 34.5 us -> 6.47 us
  waiting for transfers between devices: 161 us -> 149 us
    ppermute x16 -> x0, waiting for transfers between devices: 160 us -> none  [shift(): lax.ppermute(values, axis, pairs if way > 0 else [(b, a) for a, b in pairs])]
    all_to_all x1, waiting for transfers between devices: 0.01 us -> 149 us  [local(): exchange(packed.reshape(devices, slot_count, side, side))]
    ppermute x16 -> x0, starting transfers between devices: 84.7 us -> none  [shift(): lax.ppermute(values, axis, pairs if way > 0 else [(b, a) for a, b in pairs])]
    pallas_call x2 -> x5, Pallas kernels: 21.8 us -> 59.6 us  [the longest x3 42.9 us: rim_call(): pl.pallas_call(kernel, out_shape=shapes, in_specs=[held] * len(args), out...]
    slice x20 -> x0, local copies, waits for them, and re-layouts: 19.7 us -> none  [the longest x6 6.92 us: gathered(): lax.slice_in_dim(total, side + PAD, ext, axis=dim).astype(jnp.bfloat16)]
    concatenate x6 -> x0, other arithmetic: 10.4 us -> none  [the longest x4 7.13 us: widened(): jnp.concatenate([cells, shift(tail, axis, 1), shift(head, axis, -1)], axi...]
    add x4 -> x0, other arithmetic: 9.17 us -> none  [gathered(): lax.slice_in_dim(inner, 0, PAD, axis=dim) + to_head]
    convert_element_type x4 -> x0, local copies, waits for them, and re-layouts: 8.57 us -> none  [the longest x2 5.24 us: gathered(): to_tail = shift(before, axis, -1).astype(jnp.float32)]
  transfers between devices with their start and end apart: 18 -> 2, of which waited for: 10 -> 1; matrix products, arithmetic and copies ran while one was open for 6% -> 0% of each run, Pallas kernels for 9% -> 17%
where the time goes in v2:
time: 323 us; the launch traced here: 322 us
  Pallas kernels  152 us (47%)
  waiting for transfers between devices  149 us (46%)
  starting transfers between devices  12 us (4%)
  other arithmetic  6.47 us (2%)
    all_to_all x1, waiting for transfers between devices, local(): exchange(packed.reshape(devices, slot_count, side, side))  149 us
    pallas_call x3, Pallas kernels, rim_call(): pl.pallas_call(kernel, out_shape=shapes, in_specs=[held] * len(args), out...  42.9 us
    pallas_call x2, Pallas kernels, sides(): pl.pallas_call(sides_kernel, out_shape=jax.ShapeDtypeStruct((views, plane...  25.5 us
    pallas_call x2, Pallas kernels, depth(): pl.pallas_call(depth_kernel, out_shape=jax.ShapeDtypeStruct(along.shape,...  24.4 us
    pallas_call x1, Pallas kernels, bands(): pl.pallas_call(functools.partial(bands_kernel, (taps.shape[1] - 1) // 2,...  23.2 us
    pallas_call x2, Pallas kernels, spread(): pl.pallas_call(spread_kernel, out_shape=[jax.ShapeDtypeStruct((planes, si...  16.7 us
    pallas_call x1, Pallas kernels, observe(): pl.pallas_call(functools.partial(observe_kernel, chunk), out_shape=jax.Sh...  13.6 us
    all_to_all x1, starting transfers between devices, local(): got_labels = exchange(labels.reshape(devices, slot_count)).reshape(-1)  7.1 us
  transfers between devices with their start and end apart: 2, of which 1 were waited for; matrix products, arithmetic and copies ran while one was open for 0% of the time, Pallas kernels for 17%

profile of v2, /device:TPU:1, one launch (start us, length us, event | category | flops | bytes accessed | tf_op | source)
XLA Modules:
  0.0 321.7 jit_solution(9084022030886652683)
XLA Ops:
  0.0 0.9 convert_reduce_fusion.1
  0.9 0.7 multiply_add_fusion
  1.6 0.7 select_reduce_fusion
  2.3 0.7 sub.7
  3.0 7.1 %all-to-all-start = ((s32[32,1,8]{2,1,0:T(1,128)}), s32[32,1,8]{2,1,0:T(1,128)S(1)}, u32[]{:S(2)}, u32[]{:S(2)}) async-start(s32[32,1,8]{2,1,0:T(1,128)} %bitcast.1), calls=%async_computation | async-start | bytes 32768 | tf_op jit(solution)/shard_map/all_to_all | solution.py:498
  10.1 13.1 %rim_first.1.wide_ref = bf16[32,160,256]{2,1,0:T(8,128)(2,1)} custom-call(f32[32,128,128]{2,1,0:T(8,128)} %est_ref.3), custom_call_target="tpu_custom_call" | custom-call | tf_op jit(solution)/shard_map/rim_first/pallas_call | solution.py:466
  23.2 5.4 %pack.1 = bf16[256,128,128]{2,1,0:T(8,128)(2,1)} custom-call(s32[256]{0:T(256)} %get-tuple-element.44.pick_ref, bf16[128,128,128]{2,1,0:T(8,128)(2,1)} %tiles_ref.1), custom_call_target="tpu_custom_call" | custom-call | tf_op jit(solution)/shard_map/pack/pallas_call | solution.py:99
  28.7 0.0 all-to-all-done
  28.7 0.5 broadcast.27
  29.2 0.7 reduce.3
  29.9 0.1 reshape.48.label_ref
  30.0 0.0 copy-start.1
  30.0 0.0 copy-start.2
  30.0 4.9 %all-to-all-start.1 = ((bf16[32,8,128,128]{3,2,1,0:T(8,128)(2,1)}), bf16[32,8,128,128]{3,2,1,0:T(8,128)(2,1)}, u32[]{:S(2)}, u32[]{:S(2)}) async-start(bf16[32,8,128,128]{3,2,1,0:T(8,128)(2,1)} %bitcast.9), calls=%async_computation.1 | async-start | bytes 16777216 | tf_op jit(solution)/shard_map/all_to_all | solution.py:505
  34.9 0.0 copy-done.2
  35.0 0.1 fusion.3
  35.0 0.6 reshape.55.taps_ref
  35.7 23.2 %bands.1 = (bf16[256,768]{1,0:T(8,128)(2,1)}, bf16[6,128,160]{2,1,0:T(8,128)(2,1)}, bf16[6,256,256]{2,1,0:T(8,128)(2,1)}, bf16[6,256,256]{2,1,0:T(8,128)(2,1)}, ...) custom-call(f32[18,31]{1,0:T(8,128)} %reshape.55.taps_ref), custom_call_target="tpu_custom_call" | custom-call | tf_op jit(solution)/shard_map/bands/pallas_call | solution.py:76
  58.9 0.1 convert_reduce_fusion
  59.0 0.1 broadcast_in_dim.37
  59.1 12.8 %sides.2.sides_ref = bf16[6,32,128,128]{3,2,1,0:T(8,128)(2,1)} custom-call(bf16[32,160,256]{2,1,0:T(8,128)(2,1)} %rim_first.1.wide_ref, bf16[256,768]{1,0:T(8,128)(2,1)} %get-tuple-element.25.bx_ref, bf16[6,128,160]{2,1,0:T(8,128)(2,1)} %get-tuple-element.26.by_ref), custom_call_target="tpu_custom_call" | custom-call | flops 2264924160 | bytes 9437184 | tf_op jit(solution)/shard_map/sides/pallas_call | solution.py:165
  71.9 148.6 %all-to-all-done.1 = bf16[32,8,128,128]{3,2,1,0:T(8,128)(2,1)} async-done(((bf16[32,8,128,128]{3,2,1,0:T(8,128)(2,1)}), bf16[32,8,128,128]{3,2,1,0:T(8,128)(2,1)}, u32[]{:S(2)}, u32[]{:S(2)}) %all-to-all-start.1) | async-done | bytes 8388640 | tf_op jit(solution)/shard_map/all_to_all | solution.py:505
  220.4 13.6 %observe.1 = f32[192,128,128]{2,1,0:T(8,128)} custom-call(s32[256]{0:T(256)} %copy-done.1, bf16[256,128,128]{2,1,0:T(8,128)(2,1)} %bitcast.3.tiles_ref), custom_call_target="tpu_custom_call" | custom-call | tf_op jit(solution)/shard_map/observe/pallas_call | solution.py:136
  234.1 0.7 broadcast_in_dim.38.count_ref
  234.8 12.2 %depth.2.back_ref = bf16[6,32,128,128]{3,2,1,0:T(8,128)(2,1)} custom-call(bf16[6,32,128,128]{3,2,1,0:T(8,128)(2,1)} %sides.2.sides_ref, f32[6,32,128,128]{3,2,1,0:T(8,128)} %bitcast.7, f32[6,32,128]{2,1,0:T(8,128)} %broadcast_in_dim.38.count_ref, bf16[6,256,256]{2,1,0:T(8,128)(2,1)} %get-tuple-element.29.kz_ref, bf16[6,256,256]{2,1,0:T(8,128)(2,1)} %get-tuple-element.30.kf_ref), custom_call_target="tpu_custom_call" | custom-call | tf_op jit(solution)/shard_map/depth/pallas_call | solution.py:208
  247.0 8.3 %spread.2 = (f32[32,128,128]{2,1,0:T(8,128)}, bf16[32,32,128]{2,1,0:T(8,128)(2,1)}, bf16[4,160,128]{2,1,0:T(8,128)(2,1)}, bf16[4,160,128]{2,1,0:T(8,128)(2,1)}) custom-call(bf16[6,32,128,128]{3,2,1,0:T(8,128)(2,1)} %depth.2.back_ref, bf16[6,160,128]{2,1,0:T(8,128)(2,1)} %get-tuple-element.31.fy_ref, bf16[768,256]{1,0:T(8,128)(2,1)} %get-tuple-element.32.fx_ref), custom_call_target="tpu_custom_call" | custom-call | tf_op jit(solution)/shard_map/spread/pallas_call | solution.py:257
  255.3 18.2 %rim_between.1 = (f32[32,128,128]{2,1,0:T(8,128)}, bf16[32,160,256]{2,1,0:T(8,128)(2,1)}) custom-call(f32[32,128,128]{2,1,0:T(8,128)} %est_ref.3, f32[32,128,128]{2,1,0:T(8,128)} %get-tuple-element.33.in_ref, bf16[32,32,128]{2,1,0:T(8,128)(2,1)} %get-tuple-element.34.ys_ref, bf16[4,160,128]{2,1,0:T(8,128)(2,1)} %get-tuple-element.35.xl_ref, ...), custom_call_target="tpu_custom_call" | custom-call | tf_op jit(solution)/shard_map/rim_between/pallas_call | solution.py:466
  273.5 12.7 %sides.3.sides_ref = bf16[6,32,128,128]{3,2,1,0:T(8,128)(2,1)} custom-call(bf16[32,160,256]{2,1,0:T(8,128)(2,1)} %get-tuple-element.38.wide_ref, bf16[256,768]{1,0:T(8,128)(2,1)} %get-tuple-element.25.bx_ref, bf16[6,128,160]{2,1,0:T(8,128)(2,1)} %get-tuple-element.26.by_ref), custom_call_target="tpu_custom_call" | custom-call | flops 2264924160 | bytes 9437184 | tf_op jit(solution)/shard_map/sides/pallas_call | solution.py:165
  286.3 12.2 %depth.3.back_ref = bf16[6,32,128,128]{3,2,1,0:T(8,128)(2,1)} custom-call(bf16[6,32,128,128]{3,2,1,0:T(8,128)(2,1)} %sides.3.sides_ref, f32[6,32,128,128]{3,2,1,0:T(8,128)} %bitcast.8, f32[6,32,128]{2,1,0:T(8,128)} %broadcast_in_dim.38.count_ref, bf16[6,256,256]{2,1,0:T(8,128)(2,1)} %get-tuple-element.29.kz_ref, bf16[6,256,256]{2,1,0:T(8,128)(2,1)} %get-tuple-element.30.kf_ref), custom_call_target="tpu_custom_call" | custom-call | tf_op jit(solution)/shard_map/depth/pallas_call | solution.py:208
  298.5 8.3 %spread.3 = (f32[32,128,128]{2,1,0:T(8,128)}, bf16[32,32,128]{2,1,0:T(8,128)(2,1)}, bf16[4,160,128]{2,1,0:T(8,128)(2,1)}, bf16[4,160,128]{2,1,0:T(8,128)(2,1)}) custom-call(bf16[6,32,128,128]{3,2,1,0:T(8,128)(2,1)} %depth.3.back_ref, bf16[6,160,128]{2,1,0:T(8,128)(2,1)} %get-tuple-element.31.fy_ref, bf16[768,256]{1,0:T(8,128)(2,1)} %get-tuple-element.32.fx_ref), custom_call_target="tpu_custom_call" | custom-call | tf_op jit(solution)/shard_map/spread/pallas_call | solution.py:257
  306.8 11.5 %rim_last.1 = f32[32,128,128]{2,1,0:T(8,128)} custom-call(f32[32,128,128]{2,1,0:T(8,128)} %get-tuple-element.39.in_ref, bf16[32,32,128]{2,1,0:T(8,128)(2,1)} %get-tuple-element.40.ys_ref, bf16[4,160,128]{2,1,0:T(8,128)(2,1)} %get-tuple-element.41.xl_ref, bf16[4,160,128]{2,1,0:T(8,128)(2,1)} %get-tuple-element.42.xr_ref), custom_call_target="tpu_custom_call" | custom-call | tf_op jit(solution)/shard_map/rim_last/pallas_call | solution.py:466
  318.4 3.3 %multiply_multiply_fusion = f32[32,128,128]{2,1,0:T(8,128)} fusion(f32[32,128,128]{2,1,0:T(8,128)S(1)} %copy-done, f32[32,128,128]{2,1,0:T(8,128)} %rim_last.1), kind=kLoop, calls=%fused_computation.1 | loop fusion | flops 1048576 | bytes 6291456 | tf_op jit(solution)/shard_map/div | solution.py:527
  (4 shorter events, 0.0 us)
Async XLA Ops:
  3.0 25.7 %all-to-all-start = ((s32[32,1,8]{2,1,0:T(1,128)}), s32[32,1,8]{2,1,0:T(1,128)S(1)}, u32[]{:S(2)}, u32[]{:S(2)}) async-start(s32[32,1,8]{2,1,0:T(1,128)} %bitcast.1), calls=%async_computation | async-start | bytes 32768 | tf_op jit(solution)/shard_map/all_to_all | solution.py:498
  30.0 28.9 %copy-start.1 = (s32[256]{0:T(256)}, s32[256]{0:T(256)S(1)}, u32[]{:S(2)}) copy-start(s32[256]{0:T(256)S(1)} %reshape.48.label_ref) | copy-start | bytes 3076
  30.0 5.0 %copy-start.2 = (f32[6,3,31]{2,1,0:T(4,128)S(1)}, f32[6,3,31]{2,1,0:T(4,128)}, u32[]{:S(2)}) copy-start(f32[6,3,31]{2,1,0:T(4,128)} %param.8) | copy-start | bytes 6700
  30.0 190.4 %all-to-all-start.1 = ((bf16[32,8,128,128]{3,2,1,0:T(8,128)(2,1)}), bf16[32,8,128,128]{3,2,1,0:T(8,128)(2,1)}, u32[]{:S(2)}, u32[]{:S(2)}) async-start(bf16[32,8,128,128]{3,2,1,0:T(8,128)(2,1)} %bitcast.9), calls=%async_computation.1 | async-start | bytes 16777216 | tf_op jit(solution)/shard_map/all_to_all | solution.py:505
  306.8 11.6 %copy-start = (f32[32,128,128]{2,1,0:T(8,128)S(1)}, f32[32,128,128]{2,1,0:T(8,128)}, u32[]{:S(2)}) copy-start(f32[32,128,128]{2,1,0:T(8,128)} %get-tuple-element.37) | copy-start | bytes 6291460

commit v3 on v2

--- a/solution.py
+++ b/solution.py
@@ -107,46 +107,6 @@
     )(pick, tiles)
 
 
-def observe_kernel(chunk, label_ref, tiles_ref, out_ref):
-    step = pl.program_id(0)
-
-    @pl.when(step == 0)
-    def _():
-        def clear(plane, carry):
-            out_ref[plane] = jnp.zeros(out_ref.shape[1:], out_ref.dtype)
-            return carry
-
-        lax.fori_loop(0, out_ref.shape[0], clear, 0)
-
-    def add(i, carry):
-        label = label_ref[step * chunk + i]
-
-        @pl.when(label >= 0)
-        def _():
-            out_ref[label] += tiles_ref[i].astype(jnp.float32)
-
-        return carry
-
-    lax.fori_loop(0, chunk, add, 0)
-
-
-def observe(labels, tiles, slots):
-    chunk = 32
-    side = tiles.shape[1]
-    return pl.pallas_call(
-        functools.partial(observe_kernel, chunk),
-        out_shape=jax.ShapeDtypeStruct((slots, side, side), jnp.float32),
-        grid=(tiles.shape[0] // chunk,),
-        in_specs=[
-            pl.BlockSpec(memory_space=pltpu.SMEM),
-            pl.BlockSpec((chunk, side, side), lambda i: (i, 0, 0)),
-        ],
-        out_specs=pl.BlockSpec((slots, side, side), lambda i: (0, 0, 0)),
-        compiler_params=pltpu.CompilerParams(vmem_limit_bytes=VMEM),
-        name="observe",
-    )(labels, tiles)
-
-
 def sides_kernel(wide_ref, bx_ref, by_ref, out_ref):
     views, planes, side, _ = out_ref.shape
     for z in range(planes):
@@ -178,42 +138,24 @@
     )(wide, bx, by)
 
 
-def depth_kernel(sides_ref, seen_ref, count_ref, kz_ref, kf_ref, out_ref):
-    _, planes, rows, side = sides_ref.shape
+def depth(along, seen, count_ref, kz, kf, back_ref, v):
+    planes, side, _ = along.shape
     full = planes * 8
-    pairs = rows // 16
     count = jnp.broadcast_to(count_ref[0][:, None, :], (planes, 8, side)).reshape(full, side)
     count = jnp.concatenate([count, count], axis=1)
 
     def both(values):
         return jnp.concatenate([values[:, :8].reshape(full, side), values[:, 8:].reshape(full, side)], axis=1)
 
-    for p in range(pairs):
+    for p in range(side // 16):
         spot = slice(p * 16, p * 16 + 16)
-        stack = both(sides_ref[0, :, spot].astype(jnp.float32)).astype(jnp.bfloat16)
-        blur = jnp.dot(kz_ref[0], stack, preferred_element_type=jnp.float32)
-        seen = both(seen_ref[0, :, spot].astype(jnp.float32))
-        ratio = ((seen + damping) / (count * blur + damping)).astype(jnp.bfloat16)
-        back = jnp.dot(kf_ref[0], ratio, preferred_element_type=jnp.float32)
-        out_ref[0, :, spot] = jnp.concatenate(
+        stack = both(along[:, spot].astype(jnp.float32)).astype(jnp.bfloat16)
+        blur = jnp.dot(kz, stack, preferred_element_type=jnp.float32)
+        ratio = ((both(seen(spot)) + damping) / (count * blur + damping)).astype(jnp.bfloat16)
+        back = jnp.dot(kf, ratio, preferred_element_type=jnp.float32)
+        back_ref[v, :, spot] = jnp.concatenate(
             [back[:, :side].reshape(planes, 8, side), back[:, side:].reshape(planes, 8, side)], axis=1
         ).astype(jnp.bfloat16)
-
-
-def depth(along, seen, count, kz, kf):
-    views, planes, side, _ = along.shape
-    rows = 128
-    block = pl.BlockSpec((1, planes, rows, side), lambda v, i: (v, 0, i, 0))
-    per_view = lambda a: pl.BlockSpec((1,) + a.shape[1:], lambda v, i: (v,) + (0,) * (a.ndim - 1))
-    return pl.pallas_call(
-        depth_kernel,
-        out_shape=jax.ShapeDtypeStruct(along.shape, jnp.bfloat16),
-        grid=(views, side // rows),
-        in_specs=[block, block, per_view(count), per_view(kz), per_view(kf)],
-        out_specs=block,
-        compiler_params=pltpu.CompilerParams(vmem_limit_bytes=VMEM),
-        name="depth",
-    )(along, seen, count, kz, kf)
 
 
 def fold_lanes(values, start):
@@ -229,13 +171,13 @@
     return jnp.where(lane // PAD == start // PAD, pltpu.roll(held, (start - PAD * k) % 128, 1), 0.0)
 
 
-def spread_kernel(back_ref, fy_ref, fx_ref, in_ref, ys_ref, xl_ref, xr_ref):
-    views, planes, side, _ = back_ref.shape
+def spread(fold, back_ref, fy_ref, fx_ref, in_ref, ys_ref, xl_ref, xr_ref):
+    views, _, side, _ = back_ref.shape
     rims = []
-    for z in range(planes):
+    for z in range(8):
         wide = jnp.concatenate(
             [
-                jnp.dot(fy_ref[v], back_ref[v, z], preferred_element_type=jnp.float32).astype(jnp.bfloat16)
+                jnp.dot(fy_ref[v], back_ref[v, fold * 8 + z], preferred_element_type=jnp.float32).astype(jnp.bfloat16)
                 for v in range(views)
             ],
             axis=1,
@@ -248,35 +190,100 @@
     xr_ref[0] = fold_lanes(rims, PAD).astype(jnp.bfloat16)
 
 
-def spread(back, fy, fx):
-    views, planes, side, _ = back.shape
+def turn_kernel(chunk, loads, label_ref, tiles_ref, along_ref, count_ref, kz_ref, kf_ref, fy_ref, fx_ref, *outs):
+    *parts, seen_ref, back_ref, held_ref = outs
+    step = pl.program_id(0)
+    views, planes = back_ref.shape[:2]
+
+    if loads:
+        @pl.when(step == 0)
+        def _():
+            def clear(plane, carry):
+                held_ref[plane] = jnp.zeros(held_ref.shape[1:], jnp.float32)
+                return carry
+
+            lax.fori_loop(0, views * planes, clear, 0)
+
+        @pl.when(step < loads)
+        def _():
+            def add(i, carry):
+                label = label_ref[step * chunk + i]
+
+                @pl.when(label >= 0)
+                def _():
+                    held_ref[label] += tiles_ref[i].astype(jnp.float32)
+
+                return carry
+
+            lax.fori_loop(0, chunk, add, 0)
+
+    @pl.when((step >= loads) & (step < loads + views))
+    def _():
+        v = step - loads
+        if loads:
+            base = pl.multiple_of(v * planes, planes)
+            seen_ref[0] = held_ref[pl.ds(base, planes)].astype(jnp.bfloat16)
+            seen = lambda spot: held_ref[pl.ds(base, planes), spot]
+        else:
+            seen = lambda spot: seen_ref[0, :, spot].astype(jnp.float32)
+        depth(along_ref.at[0], seen, count_ref, kz_ref[0], kf_ref[0], back_ref, v)
+
+    @pl.when(step >= loads + views)
+    def _():
+        spread(step - loads - views, back_ref, fy_ref, fx_ref, *parts)
+
+
+def later_kernel(along_ref, seen_ref, count_ref, kz_ref, kf_ref, fy_ref, fx_ref, *outs):
+    *parts, back_ref = outs
+    turn_kernel(0, 0, None, None, along_ref, count_ref, kz_ref, kf_ref, fy_ref, fx_ref, *parts, seen_ref, back_ref, None)
+
+
+def turn(along, count, kz, kf, fy, fx, seen=None, labels=None, tiles=None):
+    views, planes, side, _ = along.shape
     ext = fy.shape[1]
-    chunk = 8
-    folds = planes // chunk
-    fold = pl.BlockSpec((1, ext, side), lambda i: (i, 0, 0))
+    folds = planes // 8
+    chunk = 32
+    loads = 0 if tiles is None else tiles.shape[0] // chunk
+    view = lambda i: jnp.clip(i - loads, 0, views - 1)
+    fold = lambda i: jnp.maximum(i - loads - views, 0)
+    per_view = lambda shape: pl.BlockSpec((1,) + shape[1:], lambda i: (view(i),) + (0,) * (len(shape) - 1))
+    per_fold = lambda shape: pl.BlockSpec(shape, lambda i: (fold(i), 0, 0))
+    whole = lambda shape: pl.BlockSpec(shape, lambda i: (0,) * len(shape))
+    volume = per_view(along.shape)
+    shapes = [
+        jax.ShapeDtypeStruct((planes, side, side), jnp.float32),
+        jax.ShapeDtypeStruct((planes, 2 * PAD, side), jnp.bfloat16),
+        jax.ShapeDtypeStruct((folds, ext, side), jnp.bfloat16),
+        jax.ShapeDtypeStruct((folds, ext, side), jnp.bfloat16),
+    ]
+    out_specs = [per_fold((8, side, side)), per_fold((8, 2 * PAD, side)), per_fold((1, ext, side)), per_fold((1, ext, side))]
+    filters = [per_view(count.shape), per_view(kz.shape), per_view(kf.shape), whole(fy.shape), whole(fx.shape)]
+    scratch = [pltpu.VMEM((views, planes, side, side), jnp.bfloat16)]
+    if loads:
+        shapes.append(jax.ShapeDtypeStruct(along.shape, jnp.bfloat16))
+        out_specs.append(volume)
+        in_specs = [
+            pl.BlockSpec(memory_space=pltpu.SMEM),
+            pl.BlockSpec((chunk, side, side), lambda i: (jnp.minimum(i, loads - 1), 0, 0)),
+            volume,
+        ]
+        args = [labels, tiles, along]
+        scratch.append(pltpu.VMEM((views * planes, side, side), jnp.float32))
+        kernel = functools.partial(turn_kernel, chunk, loads)
+    else:
+        in_specs = [volume, volume]
+        args = [along, seen]
+        kernel = later_kernel
     return pl.pallas_call(
-        spread_kernel,
-        out_shape=[
-            jax.ShapeDtypeStruct((planes, side, side), jnp.float32),
-            jax.ShapeDtypeStruct((planes, 2 * PAD, side), jnp.bfloat16),
-            jax.ShapeDtypeStruct((folds, ext, side), jnp.bfloat16),
-            jax.ShapeDtypeStruct((folds, ext, side), jnp.bfloat16),
-        ],
-        grid=(folds,),
-        in_specs=[
-            pl.BlockSpec((views, chunk, side, side), lambda i: (0, i, 0, 0)),
-            pl.BlockSpec(fy.shape, lambda i: (0, 0, 0)),
-            pl.BlockSpec(fx.shape, lambda i: (0, 0)),
-        ],
-        out_specs=[
-            pl.BlockSpec((chunk, side, side), lambda i: (i, 0, 0)),
-            pl.BlockSpec((chunk, 2 * PAD, side), lambda i: (i, 0, 0)),
-            fold,
-            fold,
-        ],
+        kernel,
+        out_shape=shapes,
+        grid=(loads + views + folds,),
+        in_specs=in_specs + filters,
+        out_specs=out_specs,
+        scratch_shapes=scratch,
         compiler_params=pltpu.CompilerParams(vmem_limit_bytes=VMEM),
-        name="spread",
-    )(back, fy, fx)
+        name="turn",
+    )(*args, count, kz, kf, fy, fx)
 
 
 NEAR = [(-1, 0), (1, 0), (0, -1), (0, 1), (-1, -1), (1, -1), (-1, 1), (1, 1)]
@@ -495,13 +502,15 @@
     exchange = functools.partial(
         lax.all_to_all, axis_name=("gy", "gx"), split_axis=0, concat_axis=0, tiled=True
     )
-    got_labels = exchange(labels.reshape(devices, slot_count)).reshape(-1)
+    me = lax.axis_index("gy") * lax.axis_size("gx") + lax.axis_index("gx")
+    everyones = lax.all_gather(labels.reshape(devices, slot_count), ("gy", "gx"))
+    got_labels = lax.dynamic_index_in_dim(everyones, me, axis=1, keepdims=False).reshape(-1)
     grid = (lax.axis_size("gy"), lax.axis_size("gx"))
     volume = jax.ShapeDtypeStruct(estimate.shape, jnp.float32)
     framed = jax.ShapeDtypeStruct((planes, side + 2 * PAD, 2 * side), jnp.bfloat16)
     rim, folds = rim_scratch(planes, side), fold_scratch(planes, side)
     (wide,) = rim_call(functools.partial(first_kernel, grid), "rim_first", 0, [framed], folds + rim, [estimate])
-    packed, wide, got_labels = lax.optimization_barrier((packed, wide, got_labels))
+    packed, wide = lax.optimization_barrier((packed, wide))
     got_tiles = exchange(packed.reshape(devices, slot_count, side, side)).reshape(-1, side, side)
 
     kernel = (psf / jnp.sum(psf, axis=2, keepdims=True)).astype(jnp.bfloat16).astype(jnp.float32)
@@ -514,9 +523,9 @@
     for repeat_index in range(ITERS):
         along = sides(wide, bx, by)
         if seen is None:
-            seen = observe(got_labels, got_tiles, views * planes).reshape(views, planes, side, side)
-        back = depth(along, seen, count, kz, kf)
-        parts = spread(back, fy, fx)
+            *parts, seen = turn(along, count, kz, kf, fy, fx, labels=got_labels, tiles=got_tiles)
+        else:
+            parts = turn(along, count, kz, kf, fy, fx, seen=seen)
         if repeat_index + 1 < ITERS:
             estimate, wide = rim_call(
                 functools.partial(between_kernel, grid, views), "rim_between", 1,

time: 323 us -> 365 us (1.13)
  blocking collectives: 0 us -> 172 us
  waiting for transfers between devices: 149 us -> 0.01 us
  Pallas kernels: 152 us -> 179 us
  starting transfers between devices: 12 us -> 5.19 us
    all_gather x0 -> x1, blocking collectives: none -> 172 us  [local(): lax.all_gather(labels.reshape(devices, slot_count), ('gy', 'gx'))]
    all_to_all x1, waiting for transfers between devices: 149 us -> 0.01 us  [local(): exchange(packed.reshape(devices, slot_count, side, side))]
    pallas_call x3, Pallas kernels: 42.9 us -> 82.4 us  [rim_call(): pl.pallas_call(kernel, out_shape=shapes, in_specs=[held] * len(args), out...]
    pallas_call x5 -> x2, Pallas kernels: 54.7 us -> 42 us  [turn(): pl.pallas_call(kernel, out_shape=shapes, grid=(loads + views + folds,), i...]
    all_to_all x1 -> x0, starting transfers between devices: 7.1 us -> none  [local(): got_labels = exchange(labels.reshape(devices, slot_count)).reshape(-1)]
  transfers between devices with their start and end apart: 2 -> 1, of which waited for: 1 -> 0; matrix products, arithmetic and copies ran while one was open for 0% -> 1% of each run, Pallas kernels for 17% -> 10%
where the time goes in v3:
time: 365 us; the launch traced here: 364 us
  Pallas kernels  179 us (49%)
  blocking collectives  172 us (47%)
  starting transfers between devices  5.19 us (1%)
  other arithmetic  5.1 us (1%)
    all_gather x1, blocking collectives, local(): lax.all_gather(labels.reshape(devices, slot_count), ('gy', 'gx'))  172 us
    pallas_call x3, Pallas kernels, rim_call(): pl.pallas_call(kernel, out_shape=shapes, in_specs=[held] * len(args), out...  82.4 us
    pallas_call x2, Pallas kernels, turn(): pl.pallas_call(kernel, out_shape=shapes, grid=(loads + views + folds,), i...  42 us
    pallas_call x2, Pallas kernels, sides(): pl.pallas_call(sides_kernel, out_shape=jax.ShapeDtypeStruct((views, plane...  25.5 us
    pallas_call x1, Pallas kernels, bands(): pl.pallas_call(functools.partial(bands_kernel, (taps.shape[1] - 1) // 2,...  23.2 us
  transfers between devices with their start and end apart: 1, of which 0 were waited for; matrix products, arithmetic and copies ran while one was open for 1% of the time, Pallas kernels for 10%

profile of v3, /device:TPU:1, one launch (start us, length us, event | category | flops | bytes accessed | tf_op | source)
XLA Modules:
  0.0 363.8 jit_solution(14748705471659101163)
XLA Ops:
  0.0 0.9 convert_reduce_fusion.1
  0.9 0.0 copy-start.2
  0.9 0.0 copy-start.3
  0.9 14.4 %rim_first.1.wide_ref = bf16[32,160,256]{2,1,0:T(8,128)(2,1)} custom-call(f32[32,128,128]{2,1,0:T(8,128)} %est_ref.3), custom_call_target="tpu_custom_call" | custom-call | tf_op jit(solution)/shard_map/rim_first/pallas_call | solution.py:473
  15.3 0.0 copy-done.2
  15.3 0.0 copy-done.3
  15.4 0.7 select_reduce_fusion
  16.0 5.4 %pack.1 = bf16[256,128,128]{2,1,0:T(8,128)(2,1)} custom-call(s32[256]{0:T(256)} %get-tuple-element.43.pick_ref, bf16[128,128,128]{2,1,0:T(8,128)(2,1)} %tiles_ref.1), custom_call_target="tpu_custom_call" | custom-call | tf_op jit(solution)/shard_map/pack/pallas_call | solution.py:99
  21.5 0.0 copy-start.4
  21.5 5.2 %all-to-all-start = ((bf16[32,8,128,128]{3,2,1,0:T(8,128)(2,1)}), bf16[32,8,128,128]{3,2,1,0:T(8,128)(2,1)}, u32[]{:S(2)}, u32[]{:S(2)}) async-start(bf16[32,8,128,128]{3,2,1,0:T(8,128)(2,1)} %bitcast.5), calls=%async_computation | async-start | bytes 16777216 | tf_op jit(solution)/shard_map/all_to_all | solution.py:514
  26.7 0.1 fusion.3
  26.8 0.6 reshape.48.taps_ref
  27.4 0.1 sub.7
  27.5 0.1 copy.7
  27.6 172.4 %all_gather.3 = s32[32,32,8]{1,2,0:T(8,128)S(1)} all-gather(s32[1,32,8]{1,2,0:T(8,128)S(1)} %copy.7), channel_id=1, replica_groups=mesh['gy'=4,'gx'=8] {'gy','gx'}, dimensions={0}, use_global_device_ids=true | all-gather | bytes 33792 | tf_op jit(solution)/shard_map/all_gather | solution.py:506
  200.0 0.7 dynamic-slice_reduce_fusion
  200.7 0.1 reshape.42.label_ref
  200.7 0.0 copy-start.1
  200.8 0.1 convert_reduce_fusion
  200.9 0.1 broadcast_in_dim.36
  201.0 23.2 %bands.1 = (bf16[256,768]{1,0:T(8,128)(2,1)}, bf16[6,128,160]{2,1,0:T(8,128)(2,1)}, bf16[6,256,256]{2,1,0:T(8,128)(2,1)}, bf16[6,256,256]{2,1,0:T(8,128)(2,1)}, ...) custom-call(f32[18,31]{1,0:T(8,128)} %reshape.48.taps_ref), custom_call_target="tpu_custom_call" | custom-call | tf_op jit(solution)/shard_map/bands/pallas_call | solution.py:76
  224.2 12.7 %sides.2.along_ref = bf16[6,32,128,128]{3,2,1,0:T(8,128)(2,1)} custom-call(bf16[32,160,256]{2,1,0:T(8,128)(2,1)} %rim_first.1.wide_ref, bf16[256,768]{1,0:T(8,128)(2,1)} %get-tuple-element.26.bx_ref, bf16[6,128,160]{2,1,0:T(8,128)(2,1)} %get-tuple-element.27.by_ref), custom_call_target="tpu_custom_call" | custom-call | flops 2264924160 | bytes 9437184 | tf_op jit(solution)/shard_map/sides/pallas_call | solution.py:125
  236.9 0.0 all-to-all-done
  236.9 0.7 broadcast_in_dim.37.count_ref
  237.7 25.7 %turn.2 = (f32[32,128,128]{2,1,0:T(8,128)}, bf16[32,32,128]{2,1,0:T(8,128)(2,1)}, bf16[4,160,128]{2,1,0:T(8,128)(2,1)}, bf16[4,160,128]{2,1,0:T(8,128)(2,1)}, bf16[6,32,128,128]{3,2,1,0:T(8,128)(2,1)}) custom-call(s32[256]{0:T(256)} %copy-done.1, bf16[256,128,128]{2,1,0:T(8,128)(2,1)} %bitcast.2.tiles_ref, bf16[6,32,128,128]{3,2,1,0:T(8,128)(2,1)} %sides.2.along_ref, ...), custom_call_target="tpu_custom_call" | custom-call | tf_op jit(solution)/shard_map/turn/pallas_call | solution.py:277
  263.4 56.8 %rim_between.1 = (f32[32,128,128]{2,1,0:T(8,128)}, bf16[32,160,256]{2,1,0:T(8,128)(2,1)}) custom-call(f32[32,128,128]{2,1,0:T(8,128)} %est_ref.3, f32[32,128,128]{2,1,0:T(8,128)} %get-tuple-element.32.in_ref, bf16[32,32,128]{2,1,0:T(8,128)(2,1)} %get-tuple-element.33.ys_ref, bf16[4,160,128]{2,1,0:T(8,128)(2,1)} %get-tuple-element.34.xl_ref, ...), custom_call_target="tpu_custom_call" | custom-call | tf_op jit(solution)/shard_map/rim_between/pallas_call | solution.py:473
  320.2 12.8 %sides.3.along_ref = bf16[6,32,128,128]{3,2,1,0:T(8,128)(2,1)} custom-call(bf16[32,160,256]{2,1,0:T(8,128)(2,1)} %get-tuple-element.37.wide_ref, bf16[256,768]{1,0:T(8,128)(2,1)} %get-tuple-element.26.bx_ref, bf16[6,128,160]{2,1,0:T(8,128)(2,1)} %get-tuple-element.27.by_ref), custom_call_target="tpu_custom_call" | custom-call | flops 2264924160 | bytes 9437184 | tf_op jit(solution)/shard_map/sides/pallas_call | solution.py:125
  332.9 16.3 %turn.3 = (f32[32,128,128]{2,1,0:T(8,128)}, bf16[32,32,128]{2,1,0:T(8,128)(2,1)}, bf16[4,160,128]{2,1,0:T(8,128)(2,1)}, bf16[4,160,128]{2,1,0:T(8,128)(2,1)}) custom-call(bf16[6,32,128,128]{3,2,1,0:T(8,128)(2,1)} %sides.3.along_ref, bf16[6,32,128,128]{3,2,1,0:T(8,128)(2,1)} %get-tuple-element.38.seen_ref, f32[6,32,128]{2,1,0:T(8,128)} %broadcast_in_dim.37.count_ref, ...), custom_call_target="tpu_custom_call" | custom-call | tf_op jit(solution)/shard_map/turn/pallas_call | solution.py:277
  349.3 0.0 copy-start
  349.3 11.2 %rim_last.1 = f32[32,128,128]{2,1,0:T(8,128)} custom-call(f32[32,128,128]{2,1,0:T(8,128)} %get-tuple-element.39.in_ref, bf16[32,32,128]{2,1,0:T(8,128)(2,1)} %get-tuple-element.40.ys_ref, bf16[4,160,128]{2,1,0:T(8,128)(2,1)} %get-tuple-element.41.xl_ref, bf16[4,160,128]{2,1,0:T(8,128)(2,1)} %get-tuple-element.42.xr_ref), custom_call_target="tpu_custom_call" | custom-call | tf_op jit(solution)/shard_map/rim_last/pallas_call | solution.py:473
  360.5 0.0 copy-done
  360.5 3.3 multiply_multiply_fusion
  (4 shorter events, 0.0 us)
Async XLA Ops:
  0.9 14.4 %copy-start.2 = (s32[128,1]{0,1:T(1,128)S(1)}, s32[128,1]{0,1:T(1,128)}, u32[]{:S(2)}) copy-start(s32[128,1]{0,1:T(1,128)} %param.6) | copy-start | bytes 1540
  0.9 14.4 %copy-start.3 = (s32[128]{0:T(128)S(1)}, s32[128]{0:T(128)}, u32[]{:S(2)}) copy-start(s32[128]{0:T(128)} %param.7) | copy-start | bytes 1540
  21.5 5.2 %copy-start.4 = (f32[6,3,31]{2,1,0:T(4,128)S(1)}, f32[6,3,31]{2,1,0:T(4,128)}, u32[]{:S(2)}) copy-start(f32[6,3,31]{2,1,0:T(4,128)} %param.8) | copy-start | bytes 6700
  21.5 215.5 %all-to-all-start = ((bf16[32,8,128,128]{3,2,1,0:T(8,128)(2,1)}), bf16[32,8,128,128]{3,2,1,0:T(8,128)(2,1)}, u32[]{:S(2)}, u32[]{:S(2)}) async-start(bf16[32,8,128,128]{3,2,1,0:T(8,128)(2,1)} %bitcast.5), calls=%async_computation | async-start | bytes 16777216 | tf_op jit(solution)/shard_map/all_to_all | solution.py:514
  200.7 36.2 %copy-start.1 = (s32[256]{0:T(256)}, s32[256]{0:T(256)S(1)}, u32[]{:S(2)}) copy-start(s32[256]{0:T(256)S(1)} %reshape.42.label_ref) | copy-start | bytes 3076
  349.3 11.2 %copy-start = (f32[32,128,128]{2,1,0:T(8,128)S(1)}, f32[32,128,128]{2,1,0:T(8,128)}, u32[]{:S(2)}) copy-start(f32[32,128,128]{2,1,0:T(8,128)} %get-tuple-element.36) | copy-start | bytes 6291460

commit v4 on v3

--- a/solution.py
+++ b/solution.py
@@ -109,17 +109,21 @@
 
 def sides_kernel(wide_ref, bx_ref, by_ref, out_ref):
     views, planes, side, _ = out_ref.shape
-    for z in range(planes):
-        along_x = jnp.dot(wide_ref[z], bx_ref[...], preferred_element_type=jnp.float32).astype(jnp.bfloat16)
-        for v in range(views):
-            out_ref[v, z] = jnp.dot(
-                by_ref[v], along_x[:, v * side : (v + 1) * side], preferred_element_type=jnp.float32
-            ).astype(jnp.bfloat16)
+    along_y = [
+        jnp.dot(by_ref[...], wide_ref[z], preferred_element_type=jnp.float32).astype(jnp.bfloat16)
+        for z in range(planes)
+    ]
+    for v in range(views):
+        spot = slice(v * side, (v + 1) * side)
+        stack = jnp.concatenate([one[spot] for one in along_y], axis=0)
+        both = jnp.dot(stack, bx_ref[:, spot], preferred_element_type=jnp.float32)
+        out_ref[v] = both.astype(jnp.bfloat16).reshape(planes, side, side)
 
 
 def sides(wide, bx, by):
     planes, ext, _ = wide.shape
     views, side, _ = by.shape
+    by = by.reshape(views * side, ext)
     chunk = 4
     macs = planes * ext * ext * side * views + planes * views * side * side * ext
     return pl.pallas_call(
@@ -129,7 +133,7 @@
         in_specs=[
             pl.BlockSpec((chunk,) + wide.shape[1:], lambda i: (i, 0, 0)),
             pl.BlockSpec(bx.shape, lambda i: (0, 0)),
-            pl.BlockSpec(by.shape, lambda i: (0, 0, 0)),
+            pl.BlockSpec(by.shape, lambda i: (0, 0)),
         ],
         out_specs=pl.BlockSpec((views, chunk, side, side), lambda i: (0, i, 0, 0)),
         compiler_params=pltpu.CompilerParams(vmem_limit_bytes=VMEM),
@@ -138,21 +142,47 @@
     )(wide, bx, by)
 
 
-def depth(along, seen, count_ref, kz, kf, back_ref, v):
+def halves(values):
+    planes, _, side = values.shape
+    full = planes * 8
+    return jnp.concatenate([values[:, :8].reshape(full, side), values[:, 8:].reshape(full, side)], axis=1)
+
+
+def below(along, count_ref, kz, spot):
     planes, side, _ = along.shape
     full = planes * 8
     count = jnp.broadcast_to(count_ref[0][:, None, :], (planes, 8, side)).reshape(full, side)
-    count = jnp.concatenate([count, count], axis=1)
-
-    def both(values):
-        return jnp.concatenate([values[:, :8].reshape(full, side), values[:, 8:].reshape(full, side)], axis=1)
-
+    stack = halves(along[:, spot].astype(jnp.float32)).astype(jnp.bfloat16)
+    blur = jnp.dot(kz, stack, preferred_element_type=jnp.float32)
+    return jnp.concatenate([count, count], axis=1) * blur + damping
+
+
+def weigh_kernel(along_ref, count_ref, kz_ref, out_ref):
+    for p in range(out_ref.shape[1]):
+        out_ref[0, p] = 1.0 / below(along_ref.at[0], count_ref, kz_ref[0], slice(p * 16, p * 16 + 16))
+
+
+def weigh(along, count, kz):
+    views, planes, side, _ = along.shape
+    pairs, full = side // 16, planes * 8
+    per_view = lambda shape: pl.BlockSpec((1,) + shape[1:], lambda i: (i,) + (0,) * (len(shape) - 1))
+    shape = (views, pairs, full, 2 * side)
+    return pl.pallas_call(
+        weigh_kernel,
+        out_shape=jax.ShapeDtypeStruct(shape, jnp.float32),
+        grid=(views,),
+        in_specs=[per_view(along.shape), per_view(count.shape), per_view(kz.shape)],
+        out_specs=per_view(shape),
+        compiler_params=pltpu.CompilerParams(vmem_limit_bytes=VMEM),
+        name="weigh",
+    )(along, count, kz)
+
+
+def depth(ratio, kf, back_ref, v):
+    _, planes, side, _ = back_ref.shape
     for p in range(side // 16):
         spot = slice(p * 16, p * 16 + 16)
-        stack = both(along[:, spot].astype(jnp.float32)).astype(jnp.bfloat16)
-        blur = jnp.dot(kz, stack, preferred_element_type=jnp.float32)
-        ratio = ((both(seen(spot)) + damping) / (count * blur + damping)).astype(jnp.bfloat16)
-        back = jnp.dot(kf, ratio, preferred_element_type=jnp.float32)
+        back = jnp.dot(kf, ratio(p, spot).astype(jnp.bfloat16), preferred_element_type=jnp.float32)
         back_ref[v, :, spot] = jnp.concatenate(
             [back[:, :side].reshape(planes, 8, side), back[:, side:].reshape(planes, 8, side)], axis=1
         ).astype(jnp.bfloat16)
@@ -190,66 +220,77 @@
     xr_ref[0] = fold_lanes(rims, PAD).astype(jnp.bfloat16)
 
 
-def turn_kernel(chunk, loads, label_ref, tiles_ref, along_ref, count_ref, kz_ref, kf_ref, fy_ref, fx_ref, *outs):
+def first_turn(chunk, loads, label_ref, tiles_ref, weight_ref, kf_ref, fy_ref, fx_ref, *outs):
     *parts, seen_ref, back_ref, held_ref = outs
     step = pl.program_id(0)
     views, planes = back_ref.shape[:2]
 
-    if loads:
-        @pl.when(step == 0)
-        def _():
-            def clear(plane, carry):
-                held_ref[plane] = jnp.zeros(held_ref.shape[1:], jnp.float32)
-                return carry
-
-            lax.fori_loop(0, views * planes, clear, 0)
-
-        @pl.when(step < loads)
-        def _():
-            def add(i, carry):
-                label = label_ref[step * chunk + i]
-
-                @pl.when(label >= 0)
-                def _():
-                    held_ref[label] += tiles_ref[i].astype(jnp.float32)
-
-                return carry
-
-            lax.fori_loop(0, chunk, add, 0)
+    @pl.when(step == 0)
+    def _():
+        def clear(plane, carry):
+            held_ref[plane] = jnp.zeros(held_ref.shape[1:], jnp.float32)
+            return carry
+
+        lax.fori_loop(0, views * planes, clear, 0)
+
+    @pl.when(step < loads)
+    def _():
+        def add(i, carry):
+            label = label_ref[step * chunk + i]
+
+            @pl.when(label >= 0)
+            def _():
+                held_ref[label] += tiles_ref[i].astype(jnp.float32)
+
+            return carry
+
+        lax.fori_loop(0, chunk, add, 0)
 
     @pl.when((step >= loads) & (step < loads + views))
     def _():
         v = step - loads
-        if loads:
-            base = pl.multiple_of(v * planes, planes)
-            seen_ref[0] = held_ref[pl.ds(base, planes)].astype(jnp.bfloat16)
-            seen = lambda spot: held_ref[pl.ds(base, planes), spot]
-        else:
-            seen = lambda spot: seen_ref[0, :, spot].astype(jnp.float32)
-        depth(along_ref.at[0], seen, count_ref, kz_ref[0], kf_ref[0], back_ref, v)
+        base = pl.multiple_of(v * planes, planes)
+
+        def ratio(p, spot):
+            seen = held_ref[pl.ds(base, planes), spot]
+            seen_ref[0, :, spot] = seen.astype(jnp.bfloat16)
+            return (halves(seen) + damping) * weight_ref[0, p]
+
+        depth(ratio, kf_ref[0], back_ref, v)
 
     @pl.when(step >= loads + views)
     def _():
         spread(step - loads - views, back_ref, fy_ref, fx_ref, *parts)
 
 
-def later_kernel(along_ref, seen_ref, count_ref, kz_ref, kf_ref, fy_ref, fx_ref, *outs):
+def later_turn(along_ref, seen_ref, count_ref, kz_ref, kf_ref, fy_ref, fx_ref, *outs):
     *parts, back_ref = outs
-    turn_kernel(0, 0, None, None, along_ref, count_ref, kz_ref, kf_ref, fy_ref, fx_ref, *parts, seen_ref, back_ref, None)
-
-
-def turn(along, count, kz, kf, fy, fx, seen=None, labels=None, tiles=None):
-    views, planes, side, _ = along.shape
-    ext = fy.shape[1]
+    step = pl.program_id(0)
+    views = back_ref.shape[0]
+
+    @pl.when(step < views)
+    def _():
+        def ratio(p, spot):
+            seen = halves(seen_ref[0, :, spot].astype(jnp.float32))
+            return (seen + damping) / below(along_ref.at[0], count_ref, kz_ref[0], spot)
+
+        depth(ratio, kf_ref[0], back_ref, step)
+
+    @pl.when(step >= views)
+    def _():
+        spread(step - views, back_ref, fy_ref, fx_ref, *parts)
+
+
+def turn(args, kf, fy, fx, loads=0):
+    views, ext, side = fy.shape
+    planes = kf.shape[1] // 8
+    chunk = 32
     folds = planes // 8
-    chunk = 32
-    loads = 0 if tiles is None else tiles.shape[0] // chunk
     view = lambda i: jnp.clip(i - loads, 0, views - 1)
     fold = lambda i: jnp.maximum(i - loads - views, 0)
     per_view = lambda shape: pl.BlockSpec((1,) + shape[1:], lambda i: (view(i),) + (0,) * (len(shape) - 1))
     per_fold = lambda shape: pl.BlockSpec(shape, lambda i: (fold(i), 0, 0))
     whole = lambda shape: pl.BlockSpec(shape, lambda i: (0,) * len(shape))
-    volume = per_view(along.shape)
     shapes = [
         jax.ShapeDtypeStruct((planes, side, side), jnp.float32),
         jax.ShapeDtypeStruct((planes, 2 * PAD, side), jnp.bfloat16),
@@ -257,23 +298,22 @@
         jax.ShapeDtypeStruct((folds, ext, side), jnp.bfloat16),
     ]
     out_specs = [per_fold((8, side, side)), per_fold((8, 2 * PAD, side)), per_fold((1, ext, side)), per_fold((1, ext, side))]
-    filters = [per_view(count.shape), per_view(kz.shape), per_view(kf.shape), whole(fy.shape), whole(fx.shape)]
+    filters = [per_view(kf.shape), whole(fy.shape), whole(fx.shape)]
     scratch = [pltpu.VMEM((views, planes, side, side), jnp.bfloat16)]
     if loads:
-        shapes.append(jax.ShapeDtypeStruct(along.shape, jnp.bfloat16))
-        out_specs.append(volume)
+        volume = (views, planes, side, side)
+        shapes.append(jax.ShapeDtypeStruct(volume, jnp.bfloat16))
+        out_specs.append(per_view(volume))
         in_specs = [
             pl.BlockSpec(memory_space=pltpu.SMEM),
             pl.BlockSpec((chunk, side, side), lambda i: (jnp.minimum(i, loads - 1), 0, 0)),
-            volume,
+            per_view(args[2].shape),
         ]
-        args = [labels, tiles, along]
         scratch.append(pltpu.VMEM((views * planes, side, side), jnp.float32))
-        kernel = functools.partial(turn_kernel, chunk, loads)
+        kernel = functools.partial(first_turn, chunk, loads)
     else:
-        in_specs = [volume, volume]
-        args = [along, seen]
-        kernel = later_kernel
+        in_specs = [per_view(a.shape) for a in args]
+        kernel = later_turn
     return pl.pallas_call(
         kernel,
         out_shape=shapes,
@@ -283,7 +323,7 @@
         scratch_shapes=scratch,
         compiler_params=pltpu.CompilerParams(vmem_limit_bytes=VMEM),
         name="turn",
-    )(*args, count, kz, kf, fy, fx)
+    )(*args, kf, fy, fx)
 
 
 NEAR = [(-1, 0), (1, 0), (0, -1), (0, 1), (-1, -1), (1, -1), (-1, 1), (1, 1)]
@@ -455,14 +495,14 @@
     widen(grid, lambda z: new_ref[z], wide_ref, left, right, *again)
 
 
-def last_kernel(grid, in_ref, ys_ref, xl_ref, xr_ref, out_ref, *rim):
+def last_kernel(grid, views, est_ref, in_ref, ys_ref, xl_ref, xr_ref, out_ref, *rim):
     greet(grid)
     gather(grid, in_ref, ys_ref, xl_ref, xr_ref, *rim)
 
     def update(p, carry):
         for k in range(8):
             z = p * 8 + k
-            out_ref[z] = totals(z, p, k, in_ref, *rim[:3])
+            out_ref[z] = est_ref[z] * totals(z, p, k, in_ref, *rim[:3]) / views
         return carry
 
     lax.fori_loop(0, in_ref.shape[0] // 8, update, 0)
@@ -502,15 +542,13 @@
     exchange = functools.partial(
         lax.all_to_all, axis_name=("gy", "gx"), split_axis=0, concat_axis=0, tiled=True
     )
-    me = lax.axis_index("gy") * lax.axis_size("gx") + lax.axis_index("gx")
-    everyones = lax.all_gather(labels.reshape(devices, slot_count), ("gy", "gx"))
-    got_labels = lax.dynamic_index_in_dim(everyones, me, axis=1, keepdims=False).reshape(-1)
+    got_labels = exchange(labels.reshape(devices, slot_count)).reshape(-1)
     grid = (lax.axis_size("gy"), lax.axis_size("gx"))
     volume = jax.ShapeDtypeStruct(estimate.shape, jnp.float32)
     framed = jax.ShapeDtypeStruct((planes, side + 2 * PAD, 2 * side), jnp.bfloat16)
     rim, folds = rim_scratch(planes, side), fold_scratch(planes, side)
     (wide,) = rim_call(functools.partial(first_kernel, grid), "rim_first", 0, [framed], folds + rim, [estimate])
-    packed, wide = lax.optimization_barrier((packed, wide))
+    packed, wide, got_labels = lax.optimization_barrier((packed, wide, got_labels))
     got_tiles = exchange(packed.reshape(devices, slot_count, side, side)).reshape(-1, side, side)
 
     kernel = (psf / jnp.sum(psf, axis=2, keepdims=True)).astype(jnp.bfloat16).astype(jnp.float32)
@@ -523,17 +561,19 @@
     for repeat_index in range(ITERS):
         along = sides(wide, bx, by)
         if seen is None:
-            *parts, seen = turn(along, count, kz, kf, fy, fx, labels=got_labels, tiles=got_tiles)
+            weight = weigh(along, count, kz)
+            *parts, seen = turn([got_labels, got_tiles, weight], kf, fy, fx, got_tiles.shape[0] // 32)
         else:
-            parts = turn(along, count, kz, kf, fy, fx, seen=seen)
+            parts = turn([along, seen, count, kz], kf, fy, fx)
         if repeat_index + 1 < ITERS:
             estimate, wide = rim_call(
                 functools.partial(between_kernel, grid, views), "rim_between", 1,
                 [volume, framed], rim + folds + rim, [estimate, *parts],
             )
         else:
-            (total,) = rim_call(functools.partial(last_kernel, grid), "rim_last", 2, [volume], rim, parts)
-            estimate = estimate * total / views
+            (estimate,) = rim_call(
+                functools.partial(last_kernel, grid, views), "rim_last", 2, [volume], rim, [estimate, *parts]
+            )
     return estimate
 
 

time: 365 us -> 308 us (0.84)
  blocking collectives: 172 us -> 0 us
  waiting for transfers between devices: 0.01 us -> 140 us
  Pallas kernels: 179 us -> 145 us
  starting transfers between devices: 5.19 us -> 12 us
    all_gather x1 -> x0, blocking collectives: 172 us -> none  [local(): lax.all_gather(labels.reshape(devices, slot_count), ('gy', 'gx'))]
    all_to_all x1, waiting for transfers between devices: 0.01 us -> 140 us  [local(): exchange(packed.reshape(devices, slot_count, side, side))]
    pallas_call x3, Pallas kernels: 82.4 us -> 43.4 us  [rim_call(): pl.pallas_call(kernel, out_shape=shapes, in_specs=[held] * len(args), out...]
    pallas_call x0 -> x1, Pallas kernels: none -> 9.32 us  [weigh(): pl.pallas_call(weigh_kernel, out_shape=jax.ShapeDtypeStruct(shape, jnp.fl...]
    all_to_all x0 -> x1, starting transfers between devices: none -> 7.1 us  [local(): got_labels = exchange(labels.reshape(devices, slot_count)).reshape(-1)]
    pallas_call x2, Pallas kernels: 25.5 us -> 21.7 us  [sides(): pl.pallas_call(sides_kernel, out_shape=jax.ShapeDtypeStruct((views, plane...]
  transfers between devices with their start and end apart: 1 -> 2, of which waited for: 0 -> 1; matrix products, arithmetic and copies ran while one was open for 1% -> 1% of each run, Pallas kernels for 10% -> 20%
where the time goes in v4:
time: 308 us; the launch traced here: 307 us
  Pallas kernels  145 us (47%)
  waiting for transfers between devices  140 us (45%)
  starting transfers between devices  12 us (4%)
  local copies, waits for them, and re-layouts  5.86 us (2%)
  other arithmetic  3.2 us (1%)
    all_to_all x1, waiting for transfers between devices, local(): exchange(packed.reshape(devices, slot_count, side, side))  140 us
    pallas_call x3, Pallas kernels, rim_call(): pl.pallas_call(kernel, out_shape=shapes, in_specs=[held] * len(args), out...  43.4 us
    pallas_call x2, Pallas kernels, turn(): pl.pallas_call(kernel, out_shape=shapes, grid=(loads + views + folds,), i...  42.1 us
    pallas_call x1, Pallas kernels, bands(): pl.pallas_call(functools.partial(bands_kernel, (taps.shape[1] - 1) // 2,...  23.3 us
    pallas_call x2, Pallas kernels, sides(): pl.pallas_call(sides_kernel, out_shape=jax.ShapeDtypeStruct((views, plane...  21.7 us
    pallas_call x1, Pallas kernels, weigh(): pl.pallas_call(weigh_kernel, out_shape=jax.ShapeDtypeStruct(shape, jnp.fl...  9.32 us
    all_to_all x1, starting transfers between devices, local(): got_labels = exchange(labels.reshape(devices, slot_count)).reshape(-1)  7.1 us
  transfers between devices with their start and end apart: 2, of which 1 were waited for; matrix products, arithmetic and copies ran while one was open for 1% of the time, Pallas kernels for 20%

profile of v4, /device:TPU:1, one launch (start us, length us, event | category | flops | bytes accessed | tf_op | source)
XLA Modules:
  0.0 307.0 jit_solution(2106988017849287105)
XLA Ops:
  0.0 0.9 convert_reduce_fusion.1
  0.9 0.7 multiply_add_fusion
  1.6 0.7 select_reduce_fusion
  2.3 0.7 sub.7
  3.0 7.1 %all-to-all-start = ((s32[32,1,8]{2,1,0:T(1,128)}), s32[32,1,8]{2,1,0:T(1,128)S(1)}, u32[]{:S(2)}, u32[]{:S(2)}) async-start(s32[32,1,8]{2,1,0:T(1,128)} %bitcast.1), calls=%async_computation | async-start | bytes 32768 | tf_op jit(solution)/shard_map/all_to_all | solution.py:545
  10.1 13.1 %rim_first.1.wide_ref = bf16[32,160,256]{2,1,0:T(8,128)(2,1)} custom-call(f32[32,128,128]{2,1,0:T(8,128)} %est_ref.3), custom_call_target="tpu_custom_call" | custom-call | tf_op jit(solution)/shard_map/rim_first/pallas_call | solution.py:513
  23.2 5.5 %pack.1 = bf16[256,128,128]{2,1,0:T(8,128)(2,1)} custom-call(s32[256]{0:T(256)} %get-tuple-element.46.pick_ref, bf16[128,128,128]{2,1,0:T(8,128)(2,1)} %tiles_ref.1), custom_call_target="tpu_custom_call" | custom-call | tf_op jit(solution)/shard_map/pack/pallas_call | solution.py:99
  28.7 0.0 all-to-all-done
  28.7 0.5 broadcast.26
  29.2 0.7 reduce.3
  29.9 0.1 reshape.49.label_ref
  30.0 0.0 copy-start
  30.0 0.0 copy-start.1
  30.0 4.9 %all-to-all-start.1 = ((bf16[32,8,128,128]{3,2,1,0:T(8,128)(2,1)}), bf16[32,8,128,128]{3,2,1,0:T(8,128)(2,1)}, u32[]{:S(2)}, u32[]{:S(2)}) async-start(bf16[32,8,128,128]{3,2,1,0:T(8,128)(2,1)} %bitcast.7), calls=%async_computation.1 | async-start | bytes 16777216 | tf_op jit(solution)/shard_map/all_to_all | solution.py:552
  35.0 0.0 copy-done.1
  35.0 0.1 fusion.3
  35.1 0.6 reshape.56.taps_ref
  35.7 23.3 %bands.1 = (bf16[256,768]{1,0:T(8,128)(2,1)}, bf16[6,128,160]{2,1,0:T(8,128)(2,1)}, bf16[6,256,256]{2,1,0:T(8,128)(2,1)}, bf16[6,256,256]{2,1,0:T(8,128)(2,1)}, ...) custom-call(f32[18,31]{1,0:T(8,128)} %reshape.56.taps_ref), custom_call_target="tpu_custom_call" | custom-call | tf_op jit(solution)/shard_map/bands/pallas_call | solution.py:76
  59.0 0.0 copy-done
  59.0 0.1 convert_reduce_fusion
  59.1 0.1 broadcast_in_dim.37
  59.2 10.8 %sides.2.along_ref = bf16[6,32,128,128]{3,2,1,0:T(8,128)(2,1)} custom-call(bf16[32,160,256]{2,1,0:T(8,128)(2,1)} %rim_first.1.wide_ref, bf16[256,768]{1,0:T(8,128)(2,1)} %get-tuple-element.28.bx_ref, bf16[768,160]{1,0:T(8,128)(2,1)} %bitcast.8), custom_call_target="tpu_custom_call" | custom-call | flops 2264924160 | bytes 9437184 | tf_op jit(solution)/shard_map/sides/pallas_call | solution.py:129
  70.0 0.7 broadcast_in_dim.38.count_ref
  70.7 9.3 %weigh.1.weight_ref = f32[6,8,256,256]{3,2,1,0:T(8,128)} custom-call(bf16[6,32,128,128]{3,2,1,0:T(8,128)(2,1)} %sides.2.along_ref, f32[6,32,128]{2,1,0:T(8,128)} %broadcast_in_dim.38.count_ref, bf16[6,256,256]{2,1,0:T(8,128)(2,1)} %get-tuple-element.30.kz_ref), custom_call_target="tpu_custom_call" | custom-call | tf_op jit(solution)/shard_map/weigh/pallas_call | solution.py:170
  80.1 140.4 %all-to-all-done.1 = bf16[32,8,128,128]{3,2,1,0:T(8,128)(2,1)} async-done(((bf16[32,8,128,128]{3,2,1,0:T(8,128)(2,1)}), bf16[32,8,128,128]{3,2,1,0:T(8,128)(2,1)}, u32[]{:S(2)}, u32[]{:S(2)}) %all-to-all-start.1) | async-done | bytes 8388640 | tf_op jit(solution)/shard_map/all_to_all | solution.py:552
  220.5 25.6 %turn.2 = (f32[32,128,128]{2,1,0:T(8,128)}, bf16[32,32,128]{2,1,0:T(8,128)(2,1)}, bf16[4,160,128]{2,1,0:T(8,128)(2,1)}, bf16[4,160,128]{2,1,0:T(8,128)(2,1)}, bf16[6,32,128,128]{3,2,1,0:T(8,128)(2,1)}) custom-call(s32[256]{0:T(256)} %copy-done, bf16[256,128,128]{2,1,0:T(8,128)(2,1)} %bitcast.3.tiles_ref, f32[6,8,256,256]{3,2,1,0:T(8,128)} %weigh.1.weight_ref, ...), custom_call_target="tpu_custom_call" | custom-call | tf_op jit(solution)/shard_map/turn/pallas_call | solution.py:317
  246.1 18.2 %rim_between.1 = (f32[32,128,128]{2,1,0:T(8,128)}, bf16[32,160,256]{2,1,0:T(8,128)(2,1)}) custom-call(f32[32,128,128]{2,1,0:T(8,128)} %est_ref.3, f32[32,128,128]{2,1,0:T(8,128)} %get-tuple-element.34.in_ref, bf16[32,32,128]{2,1,0:T(8,128)(2,1)} %get-tuple-element.35.ys_ref, bf16[4,160,128]{2,1,0:T(8,128)(2,1)} %get-tuple-element.36.xl_ref, ...), custom_call_target="tpu_custom_call" | custom-call | tf_op jit(solution)/shard_map/rim_between/pallas_call | solution.py:513
  264.3 10.8 %sides.3.along_ref = bf16[6,32,128,128]{3,2,1,0:T(8,128)(2,1)} custom-call(bf16[32,160,256]{2,1,0:T(8,128)(2,1)} %get-tuple-element.39.wide_ref, bf16[256,768]{1,0:T(8,128)(2,1)} %get-tuple-element.28.bx_ref, bf16[768,160]{1,0:T(8,128)(2,1)} %bitcast.9), custom_call_target="tpu_custom_call" | custom-call | flops 2264924160 | bytes 9437184 | tf_op jit(solution)/shard_map/sides/pallas_call | solution.py:129
  275.2 16.5 %turn.3 = (f32[32,128,128]{2,1,0:T(8,128)}, bf16[32,32,128]{2,1,0:T(8,128)(2,1)}, bf16[4,160,128]{2,1,0:T(8,128)(2,1)}, bf16[4,160,128]{2,1,0:T(8,128)(2,1)}) custom-call(bf16[6,32,128,128]{3,2,1,0:T(8,128)(2,1)} %sides.3.along_ref, bf16[6,32,128,128]{3,2,1,0:T(8,128)(2,1)} %get-tuple-element.40.seen_ref, f32[6,32,128]{2,1,0:T(8,128)} %broadcast_in_dim.38.count_ref, ...), custom_call_target="tpu_custom_call" | custom-call | tf_op jit(solution)/shard_map/turn/pallas_call | solution.py:317
  291.7 12.1 %rim_last.1 = f32[32,128,128]{2,1,0:T(8,128)} custom-call(f32[32,128,128]{2,1,0:T(8,128)} %get-tuple-element.38.est_ref, f32[32,128,128]{2,1,0:T(8,128)} %get-tuple-element.41.in_ref, bf16[32,32,128]{2,1,0:T(8,128)(2,1)} %get-tuple-element.42.ys_ref, bf16[4,160,128]{2,1,0:T(8,128)(2,1)} %get-tuple-element.43.xl_ref, ...), custom_call_target="tpu_custom_call" | custom-call | tf_op jit(solution)/shard_map/rim_last/pallas_call | solution.py:513
  303.8 3.1 %copy.9 = f32[32,128,128]{2,1,0:T(8,128)} copy(f32[32,128,128]{2,1,0:T(8,128)} %rim_last.1) | data formatting | bytes 4194304
  (1 shorter events, 0.0 us)
Async XLA Ops:
  3.0 25.7 %all-to-all-start = ((s32[32,1,8]{2,1,0:T(1,128)}), s32[32,1,8]{2,1,0:T(1,128)S(1)}, u32[]{:S(2)}, u32[]{:S(2)}) async-start(s32[32,1,8]{2,1,0:T(1,128)} %bitcast.1), calls=%async_computation | async-start | bytes 32768 | tf_op jit(solution)/shard_map/all_to_all | solution.py:545
  30.0 29.0 %copy-start = (s32[256]{0:T(256)}, s32[256]{0:T(256)S(1)}, u32[]{:S(2)}) copy-start(s32[256]{0:T(256)S(1)} %reshape.49.label_ref) | copy-start | bytes 3076
  30.0 5.0 %copy-start.1 = (f32[6,3,31]{2,1,0:T(4,128)S(1)}, f32[6,3,31]{2,1,0:T(4,128)}, u32[]{:S(2)}) copy-start(f32[6,3,31]{2,1,0:T(4,128)} %param.8) | copy-start | bytes 6700
  30.0 190.4 %all-to-all-start.1 = ((bf16[32,8,128,128]{3,2,1,0:T(8,128)(2,1)}), bf16[32,8,128,128]{3,2,1,0:T(8,128)(2,1)}, u32[]{:S(2)}, u32[]{:S(2)}) async-start(bf16[32,8,128,128]{3,2,1,0:T(8,128)(2,1)} %bitcast.7), calls=%async_computation.1 | async-start | bytes 16777216 | tf_op jit(solution)/shard_map/all_to_all | solution.py:552

commit v5 on v4

--- a/solution.py
+++ b/solution.py
@@ -231,20 +231,17 @@
             held_ref[plane] = jnp.zeros(held_ref.shape[1:], jnp.float32)
             return carry
 
-        lax.fori_loop(0, views * planes, clear, 0)
+        lax.fori_loop(0, views * planes + 1, clear, 0)
 
     @pl.when(step < loads)
     def _():
         def add(i, carry):
             label = label_ref[step * chunk + i]
-
-            @pl.when(label >= 0)
-            def _():
-                held_ref[label] += tiles_ref[i].astype(jnp.float32)
-
+            spot = jnp.where(label < 0, views * planes, label)
+            held_ref[spot] += tiles_ref[i].astype(jnp.float32)
             return carry
 
-        lax.fori_loop(0, chunk, add, 0)
+        lax.fori_loop(0, chunk, add, 0, unroll=4)
 
     @pl.when((step >= loads) & (step < loads + views))
     def _():
@@ -309,7 +306,7 @@
             pl.BlockSpec((chunk, side, side), lambda i: (jnp.minimum(i, loads - 1), 0, 0)),
             per_view(args[2].shape),
         ]
-        scratch.append(pltpu.VMEM((views * planes, side, side), jnp.float32))
+        scratch.append(pltpu.VMEM((views * planes + 1, side, side), jnp.float32))
         kernel = functools.partial(first_turn, chunk, loads)
     else:
         in_specs = [per_view(a.shape) for a in args]
@@ -352,27 +349,30 @@
     pl.semaphore_wait(barrier, tall * broad - 1)
 
 
-def swap(grid, moves, send_sems, recv_sems):
-    def copy(i, where):
-        source, dest = moves[i]
-        return pltpu.make_async_remote_copy(
-            src_ref=source, dst_ref=dest, send_sem=send_sems.at[i], recv_sem=recv_sems.at[i],
-            device_id=where, device_id_type=pl.DeviceIdType.MESH,
-        )
-
-    for i, (dy, dx) in enumerate(NEAR):
-        there, where = inside(grid, dy, dx)
+def move(i, where, moves, send_sems, recv_sems):
+    source, dest = moves[i]
+    return pltpu.make_async_remote_copy(
+        src_ref=source, dst_ref=dest, send_sem=send_sems.at[i], recv_sem=recv_sems.at[i],
+        device_id=where, device_id_type=pl.DeviceIdType.MESH,
+    )
+
+
+def launch(grid, which, moves, send_sems, recv_sems):
+    for i in which:
+        there, where = inside(grid, *NEAR[i])
 
         @pl.when(there)
         def _():
-            copy(i, where).start()
-
+            move(i, where, moves, send_sems, recv_sems).start()
+
+
+def land(grid, moves, send_sems, recv_sems):
     for i, (dy, dx) in enumerate(NEAR):
         there, where = inside(grid, -dy, -dx)
 
         @pl.when(there)
         def _():
-            copy(i, where).wait_recv()
+            move(i, where, moves, send_sems, recv_sems).wait_recv()
 
         @pl.when(jnp.logical_not(there))
         def _():
@@ -384,24 +384,13 @@
 
         @pl.when(there)
         def _():
-            copy(i, where).wait_send()
+            move(i, where, moves, send_sems, recv_sems).wait_send()
 
 
 def widen(grid, fresh, wide_ref, left, right, rows, from_left, from_right, send_sems, recv_sems):
     planes, ext, _ = wide_ref.shape
     side = ext - 2 * PAD
 
-    def cut(p, carry):
-        values = []
-        for k in range(8):
-            plane = fresh(p * 8 + k)
-            values.append(plane)
-            wide_ref[p * 8 + k, :side, :side] = plane.astype(jnp.bfloat16)
-        left[p] = fold_lanes(values, 0).astype(jnp.bfloat16)
-        right[p] = fold_lanes(values, side - PAD).astype(jnp.bfloat16)
-        return carry
-
-    lax.fori_loop(0, planes // 8, cut, 0)
     first, last = pl.ds(0, PAD), pl.ds(side - PAD, PAD)
     whole, before, after = pl.ds(0, side), pl.ds(side, PAD), pl.ds(side + PAD, PAD)
     lanes = pl.ds(0, side)
@@ -415,7 +404,23 @@
         (right.at[:, first], from_left.at[:, after]),
         (right.at[:, last], from_left.at[:, before]),
     ]
-    swap(grid, moves, send_sems, recv_sems)
+
+    def cast(z, carry):
+        wide_ref[z, :side, :side] = fresh(z).astype(jnp.bfloat16)
+        return carry
+
+    lax.fori_loop(0, planes, cast, 0, unroll=4)
+    launch(grid, (0, 1), moves, send_sems, recv_sems)
+
+    def cut(p, carry):
+        values = [fresh(p * 8 + k) for k in range(8)]
+        left[p] = fold_lanes(values, 0).astype(jnp.bfloat16)
+        right[p] = fold_lanes(values, side - PAD).astype(jnp.bfloat16)
+        return carry
+
+    lax.fori_loop(0, planes // 8, cut, 0)
+    launch(grid, range(2, 8), moves, send_sems, recv_sems)
+    land(grid, moves, send_sems, recv_sems)
 
     def paste(p, carry):
         low = from_left[p].astype(jnp.float32)
@@ -458,7 +463,8 @@
         (xr_ref.at[:, before], from_left.at[:, after]),
         (xr_ref.at[:, after], from_left.at[:, before]),
     ]
-    swap(grid, moves, send_sems, recv_sems)
+    launch(grid, range(8), moves, send_sems, recv_sems)
+    land(grid, moves, send_sems, recv_sems)
 
 
 def totals(z, p, k, in_ref, rows, from_left, from_right):
@@ -547,12 +553,14 @@
     volume = jax.ShapeDtypeStruct(estimate.shape, jnp.float32)
     framed = jax.ShapeDtypeStruct((planes, side + 2 * PAD, 2 * side), jnp.bfloat16)
     rim, folds = rim_scratch(planes, side), fold_scratch(planes, side)
-    (wide,) = rim_call(functools.partial(first_kernel, grid), "rim_first", 0, [framed], folds + rim, [estimate])
-    packed, wide, got_labels = lax.optimization_barrier((packed, wide, got_labels))
+    packed, psf, got_labels = lax.optimization_barrier((packed, psf, got_labels))
     got_tiles = exchange(packed.reshape(devices, slot_count, side, side)).reshape(-1, side, side)
 
     kernel = (psf / jnp.sum(psf, axis=2, keepdims=True)).astype(jnp.bfloat16).astype(jnp.float32)
     bx, by, kz, kf, fy, fx = bands(kernel.reshape(views * 3, taps), planes, side)
+
+    bx, start = lax.optimization_barrier((bx, estimate))
+    (wide,) = rim_call(functools.partial(first_kernel, grid), "rim_first", 0, [framed], folds + rim, [start])
 
     sorting = got_labels[None, :] == jnp.arange(views * planes)[:, None]
     counted = jnp.sum(sorting.astype(jnp.float32), axis=1).reshape(views, planes)

time: 308 us -> 322 us (1.045)
  Pallas kernels: 145 us -> 277 us
  waiting for transfers between devices: 140 us -> 23.2 us
    pallas_call x3, Pallas kernels: 43.4 us -> 176 us  [rim_call(): pl.pallas_call(kernel, out_shape=shapes, in_specs=[held] * len(args), out...]
    all_to_all x1, waiting for transfers between devices: 140 us -> 22 us  [local(): exchange(packed.reshape(devices, slot_count, side, side))]
  transfers between devices with their start and end apart: 2 -> 2, of which waited for: 1 -> 2; matrix products, arithmetic and copies ran while one was open for 1% -> 1% of each run, Pallas kernels for 20% -> 52%
where the time goes in v5:
time: 322 us; the launch traced here: 321 us
  Pallas kernels  277 us (86%)
  waiting for transfers between devices  23.2 us (7%)
  starting transfers between devices  11.8 us (4%)
  local copies, waits for them, and re-layouts  5.86 us (2%)
  other arithmetic  3.22 us (1%)
    pallas_call x3, Pallas kernels, rim_call(): pl.pallas_call(kernel, out_shape=shapes, in_specs=[held] * len(args), out...  176 us
    pallas_call x2, Pallas kernels, turn(): pl.pallas_call(kernel, out_shape=shapes, grid=(loads + views + folds,), i...  40.8 us
    pallas_call x1, Pallas kernels, bands(): pl.pallas_call(functools.partial(bands_kernel, (taps.shape[1] - 1) // 2,...  23.3 us
    all_to_all x1, waiting for transfers between devices, local(): exchange(packed.reshape(devices, slot_count, side, side))  22 us
    pallas_call x2, Pallas kernels, sides(): pl.pallas_call(sides_kernel, out_shape=jax.ShapeDtypeStruct((views, plane...  21.7 us
    pallas_call x1, Pallas kernels, weigh(): pl.pallas_call(weigh_kernel, out_shape=jax.ShapeDtypeStruct(shape, jnp.fl...  9.32 us
    all_to_all x1, starting transfers between devices, local(): got_labels = exchange(labels.reshape(devices, slot_count)).reshape(-1)  7.1 us
  transfers between devices with their start and end apart: 2, of which 2 were waited for; matrix products, arithmetic and copies ran while one was open for 1% of the time, Pallas kernels for 52%

profile of v5, /device:TPU:1, one launch (start us, length us, event | category | flops | bytes accessed | tf_op | source)
XLA Modules:
  0.0 320.8 jit_solution(11983360768206072799)
XLA Ops:
  0.0 0.9 convert_reduce_fusion.1
  0.9 0.7 multiply_add_fusion
  1.6 0.7 select_reduce_fusion
  2.3 0.7 sub.7
  3.0 7.1 %all-to-all-start = ((s32[32,1,8]{2,1,0:T(1,128)}), s32[32,1,8]{2,1,0:T(1,128)S(1)}, u32[]{:S(2)}, u32[]{:S(2)}) async-start(s32[32,1,8]{2,1,0:T(1,128)} %bitcast.1), calls=%async_computation | async-start | bytes 32768 | tf_op jit(solution)/shard_map/all_to_all | solution.py:551
  10.1 5.5 %pack.1 = bf16[256,128,128]{2,1,0:T(8,128)(2,1)} custom-call(s32[256]{0:T(256)} %get-tuple-element.50.pick_ref, bf16[128,128,128]{2,1,0:T(8,128)(2,1)} %tiles_ref.1), custom_call_target="tpu_custom_call" | custom-call | tf_op jit(solution)/shard_map/pack/pallas_call | solution.py:99
  15.6 1.2 all-to-all-done
  16.8 0.5 broadcast.26
  17.3 0.7 reduce.3
  18.0 0.1 reshape.49.label_ref
  18.1 0.0 copy-start
  18.1 0.0 copy-start.1
  18.1 4.7 %all-to-all-start.1 = ((bf16[32,8,128,128]{3,2,1,0:T(8,128)(2,1)}), bf16[32,8,128,128]{3,2,1,0:T(8,128)(2,1)}, u32[]{:S(2)}, u32[]{:S(2)}) async-start(bf16[32,8,128,128]{3,2,1,0:T(8,128)(2,1)} %bitcast.7), calls=%async_computation.1 | async-start | bytes 16777216 | tf_op jit(solution)/shard_map/all_to_all | solution.py:557
  22.9 0.0 copy-done
  22.9 0.1 convert_reduce_fusion
  23.0 0.1 broadcast_in_dim.37
  23.1 0.0 copy-done.1
  23.1 0.1 fusion.3
  23.2 0.6 reshape.56.taps_ref
  23.8 23.3 %bands.1 = (bf16[256,768]{1,0:T(8,128)(2,1)}, bf16[6,128,160]{2,1,0:T(8,128)(2,1)}, bf16[6,256,256]{2,1,0:T(8,128)(2,1)}, bf16[6,256,256]{2,1,0:T(8,128)(2,1)}, ...) custom-call(f32[18,31]{1,0:T(8,128)} %reshape.56.taps_ref), custom_call_target="tpu_custom_call" | custom-call | tf_op jit(solution)/shard_map/bands/pallas_call | solution.py:76
  47.1 118.8 %rim_first.1.wide_ref = bf16[32,160,256]{2,1,0:T(8,128)(2,1)} custom-call(f32[32,128,128]{2,1,0:T(8,128)} %est_ref.2), custom_call_target="tpu_custom_call" | custom-call | tf_op jit(solution)/shard_map/rim_first/pallas_call | solution.py:519
  165.9 10.8 %sides.2.along_ref = bf16[6,32,128,128]{3,2,1,0:T(8,128)(2,1)} custom-call(bf16[32,160,256]{2,1,0:T(8,128)(2,1)} %rim_first.1.wide_ref, bf16[256,768]{1,0:T(8,128)(2,1)} %get-tuple-element.32.bx_ref, bf16[768,160]{1,0:T(8,128)(2,1)} %bitcast.8), custom_call_target="tpu_custom_call" | custom-call | flops 2264924160 | bytes 9437184 | tf_op jit(solution)/shard_map/sides/pallas_call | solution.py:129
  176.8 0.7 broadcast_in_dim.38.count_ref
  177.5 9.3 %weigh.1.weight_ref = f32[6,8,256,256]{3,2,1,0:T(8,128)} custom-call(bf16[6,32,128,128]{3,2,1,0:T(8,128)(2,1)} %sides.2.along_ref, f32[6,32,128]{2,1,0:T(8,128)} %broadcast_in_dim.38.count_ref, bf16[6,256,256]{2,1,0:T(8,128)(2,1)} %get-tuple-element.34.kz_ref), custom_call_target="tpu_custom_call" | custom-call | tf_op jit(solution)/shard_map/weigh/pallas_call | solution.py:170
  186.8 22.0 %all-to-all-done.1 = bf16[32,8,128,128]{3,2,1,0:T(8,128)(2,1)} async-done(((bf16[32,8,128,128]{3,2,1,0:T(8,128)(2,1)}), bf16[32,8,128,128]{3,2,1,0:T(8,128)(2,1)}, u32[]{:S(2)}, u32[]{:S(2)}) %all-to-all-start.1) | async-done | bytes 8388640 | tf_op jit(solution)/shard_map/all_to_all | solution.py:557
  208.9 24.2 %turn.2 = (f32[32,128,128]{2,1,0:T(8,128)}, bf16[32,32,128]{2,1,0:T(8,128)(2,1)}, bf16[4,160,128]{2,1,0:T(8,128)(2,1)}, bf16[4,160,128]{2,1,0:T(8,128)(2,1)}, bf16[6,32,128,128]{3,2,1,0:T(8,128)(2,1)}) custom-call(s32[256]{0:T(256)} %copy-done, bf16[256,128,128]{2,1,0:T(8,128)(2,1)} %bitcast.3.tiles_ref, f32[6,8,256,256]{3,2,1,0:T(8,128)} %weigh.1.weight_ref, ...), custom_call_target="tpu_custom_call" | custom-call | tf_op jit(solution)/shard_map/turn/pallas_call | solution.py:314
  233.1 45.2 %rim_between.1 = (f32[32,128,128]{2,1,0:T(8,128)}, bf16[32,160,256]{2,1,0:T(8,128)(2,1)}) custom-call(f32[32,128,128]{2,1,0:T(8,128)} %est_ref.2, f32[32,128,128]{2,1,0:T(8,128)} %get-tuple-element.38.in_ref, bf16[32,32,128]{2,1,0:T(8,128)(2,1)} %get-tuple-element.39.ys_ref, bf16[4,160,128]{2,1,0:T(8,128)(2,1)} %get-tuple-element.40.xl_ref, ...), custom_call_target="tpu_custom_call" | custom-call | tf_op jit(solution)/shard_map/rim_between/pallas_call | solution.py:519
  278.4 10.8 %sides.3.along_ref = bf16[6,32,128,128]{3,2,1,0:T(8,128)(2,1)} custom-call(bf16[32,160,256]{2,1,0:T(8,128)(2,1)} %get-tuple-element.43.wide_ref, bf16[256,768]{1,0:T(8,128)(2,1)} %get-tuple-element.32.bx_ref, bf16[768,160]{1,0:T(8,128)(2,1)} %bitcast.9), custom_call_target="tpu_custom_call" | custom-call | flops 2264924160 | bytes 9437184 | tf_op jit(solution)/shard_map/sides/pallas_call | solution.py:129
  289.2 16.5 %turn.3 = (f32[32,128,128]{2,1,0:T(8,128)}, bf16[32,32,128]{2,1,0:T(8,128)(2,1)}, bf16[4,160,128]{2,1,0:T(8,128)(2,1)}, bf16[4,160,128]{2,1,0:T(8,128)(2,1)}) custom-call(bf16[6,32,128,128]{3,2,1,0:T(8,128)(2,1)} %sides.3.along_ref, bf16[6,32,128,128]{3,2,1,0:T(8,128)(2,1)} %get-tuple-element.44.seen_ref, f32[6,32,128]{2,1,0:T(8,128)} %broadcast_in_dim.38.count_ref, ...), custom_call_target="tpu_custom_call" | custom-call | tf_op jit(solution)/shard_map/turn/pallas_call | solution.py:314
  305.8 11.9 %rim_last.1 = f32[32,128,128]{2,1,0:T(8,128)} custom-call(f32[32,128,128]{2,1,0:T(8,128)} %get-tuple-element.42.est_ref, f32[32,128,128]{2,1,0:T(8,128)} %get-tuple-element.45.in_ref, bf16[32,32,128]{2,1,0:T(8,128)(2,1)} %get-tuple-element.46.ys_ref, bf16[4,160,128]{2,1,0:T(8,128)(2,1)} %get-tuple-element.47.xl_ref, ...), custom_call_target="tpu_custom_call" | custom-call | tf_op jit(solution)/shard_map/rim_last/pallas_call | solution.py:519
  317.6 3.1 copy.9
  (1 shorter events, 0.0 us)
Async XLA Ops:
  3.0 13.8 %all-to-all-start = ((s32[32,1,8]{2,1,0:T(1,128)}), s32[32,1,8]{2,1,0:T(1,128)S(1)}, u32[]{:S(2)}, u32[]{:S(2)}) async-start(s32[32,1,8]{2,1,0:T(1,128)} %bitcast.1), calls=%async_computation | async-start | bytes 32768 | tf_op jit(solution)/shard_map/all_to_all | solution.py:551
  18.1 4.7 %copy-start = (s32[256]{0:T(256)}, s32[256]{0:T(256)S(1)}, u32[]{:S(2)}) copy-start(s32[256]{0:T(256)S(1)} %reshape.49.label_ref) | copy-start | bytes 3076
  18.1 4.9 %copy-start.1 = (f32[6,3,31]{2,1,0:T(4,128)S(1)}, f32[6,3,31]{2,1,0:T(4,128)}, u32[]{:S(2)}) copy-start(f32[6,3,31]{2,1,0:T(4,128)} %param.8) | copy-start | bytes 6700
  18.1 190.7 %all-to-all-start.1 = ((bf16[32,8,128,128]{3,2,1,0:T(8,128)(2,1)}), bf16[32,8,128,128]{3,2,1,0:T(8,128)(2,1)}, u32[]{:S(2)}, u32[]{:S(2)}) async-start(bf16[32,8,128,128]{3,2,1,0:T(8,128)(2,1)} %bitcast.7), calls=%async_computation.1 | async-start | bytes 16777216 | tf_op jit(solution)/shard_map/all_to_all | solution.py:557

commit v6 on v5

--- a/solution.py
+++ b/solution.py
@@ -553,14 +553,12 @@
     volume = jax.ShapeDtypeStruct(estimate.shape, jnp.float32)
     framed = jax.ShapeDtypeStruct((planes, side + 2 * PAD, 2 * side), jnp.bfloat16)
     rim, folds = rim_scratch(planes, side), fold_scratch(planes, side)
-    packed, psf, got_labels = lax.optimization_barrier((packed, psf, got_labels))
+    (wide,) = rim_call(functools.partial(first_kernel, grid), "rim_first", 0, [framed], folds + rim, [estimate])
+    packed, psf, got_labels, wide = lax.optimization_barrier((packed, psf, got_labels, wide))
     got_tiles = exchange(packed.reshape(devices, slot_count, side, side)).reshape(-1, side, side)
 
     kernel = (psf / jnp.sum(psf, axis=2, keepdims=True)).astype(jnp.bfloat16).astype(jnp.float32)
     bx, by, kz, kf, fy, fx = bands(kernel.reshape(views * 3, taps), planes, side)
-
-    bx, start = lax.optimization_barrier((bx, estimate))
-    (wide,) = rim_call(functools.partial(first_kernel, grid), "rim_first", 0, [framed], folds + rim, [start])
 
     sorting = got_labels[None, :] == jnp.arange(views * planes)[:, None]
     counted = jnp.sum(sorting.astype(jnp.float32), axis=1).reshape(views, planes)

time: 322 us -> 306 us (0.950)
  Pallas kernels: 277 us -> 143 us
  waiting for transfers between devices: 23.2 us -> 140 us
    pallas_call x3, Pallas kernels: 176 us -> 42.4 us  [rim_call(): pl.pallas_call(kernel, out_shape=shapes, in_specs=[held] * len(args), out...]
    all_to_all x1, waiting for transfers between devices: 22 us -> 140 us  [local(): exchange(packed.reshape(devices, slot_count, side, side))]
  transfers between devices with their start and end apart: 2 -> 2, of which waited for: 2 -> 1; matrix products, arithmetic and copies ran while one was open for 1% -> 1% of each run, Pallas kernels for 52% -> 20%
where the time goes in v6:
time: 306 us; the launch traced here: 305 us
  Pallas kernels  143 us (47%)
  waiting for transfers between devices  140 us (46%)
  starting transfers between devices  12 us (4%)
  local copies, waits for them, and re-layouts  5.86 us (2%)
  other arithmetic  3.2 us (1%)
    all_to_all x1, waiting for transfers between devices, local(): exchange(packed.reshape(devices, slot_count, side, side))  140 us
    pallas_call x3, Pallas kernels, rim_call(): pl.pallas_call(kernel, out_shape=shapes, in_specs=[held] * len(args), out...  42.4 us
    pallas_call x2, Pallas kernels, turn(): pl.pallas_call(kernel, out_shape=shapes, grid=(loads + views + folds,), i...  40.9 us
    pallas_call x1, Pallas kernels, bands(): pl.pallas_call(functools.partial(bands_kernel, (taps.shape[1] - 1) // 2,...  23.3 us
    pallas_call x2, Pallas kernels, sides(): pl.pallas_call(sides_kernel, out_shape=jax.ShapeDtypeStruct((views, plane...  21.7 us
    pallas_call x1, Pallas kernels, weigh(): pl.pallas_call(weigh_kernel, out_shape=jax.ShapeDtypeStruct(shape, jnp.fl...  9.32 us
    all_to_all x1, starting transfers between devices, local(): got_labels = exchange(labels.reshape(devices, slot_count)).reshape(-1)  7.1 us
  transfers between devices with their start and end apart: 2, of which 1 were waited for; matrix products, arithmetic and copies ran while one was open for 1% of the time, Pallas kernels for 20%

profile of v6, /device:TPU:1, one launch (start us, length us, event | category | flops | bytes accessed | tf_op | source)
XLA Modules:
  0.0 304.7 jit_solution(17875363699925962420)
XLA Ops:
  0.0 0.9 convert_reduce_fusion.1
  0.9 0.7 multiply_add_fusion
  1.6 0.7 select_reduce_fusion
  2.3 0.7 sub.7
  3.0 7.1 %all-to-all-start = ((s32[32,1,8]{2,1,0:T(1,128)}), s32[32,1,8]{2,1,0:T(1,128)S(1)}, u32[]{:S(2)}, u32[]{:S(2)}) async-start(s32[32,1,8]{2,1,0:T(1,128)} %bitcast.1), calls=%async_computation | async-start | bytes 32768 | tf_op jit(solution)/shard_map/all_to_all | solution.py:551
  10.1 12.4 %rim_first.1.wide_ref = bf16[32,160,256]{2,1,0:T(8,128)(2,1)} custom-call(f32[32,128,128]{2,1,0:T(8,128)} %est_ref.3), custom_call_target="tpu_custom_call" | custom-call | tf_op jit(solution)/shard_map/rim_first/pallas_call | solution.py:519
  22.5 5.5 %pack.1 = bf16[256,128,128]{2,1,0:T(8,128)(2,1)} custom-call(s32[256]{0:T(256)} %get-tuple-element.48.pick_ref, bf16[128,128,128]{2,1,0:T(8,128)(2,1)} %tiles_ref.1), custom_call_target="tpu_custom_call" | custom-call | tf_op jit(solution)/shard_map/pack/pallas_call | solution.py:99
  28.0 0.0 all-to-all-done
  28.0 0.5 broadcast.26
  28.6 0.7 reduce.3
  29.3 0.1 reshape.49.label_ref
  29.3 0.0 copy-start
  29.3 0.0 copy-start.1
  29.4 4.9 %all-to-all-start.1 = ((bf16[32,8,128,128]{3,2,1,0:T(8,128)(2,1)}), bf16[32,8,128,128]{3,2,1,0:T(8,128)(2,1)}, u32[]{:S(2)}, u32[]{:S(2)}) async-start(bf16[32,8,128,128]{3,2,1,0:T(8,128)(2,1)} %bitcast.7), calls=%async_computation.1 | async-start | bytes 16777216 | tf_op jit(solution)/shard_map/all_to_all | solution.py:558
  34.3 0.0 copy-done
  34.3 0.1 convert_reduce_fusion
  34.4 0.1 broadcast_in_dim.37
  34.5 0.0 copy-done.1
  34.5 0.1 fusion.3
  34.6 0.6 reshape.56.taps_ref
  35.2 23.3 %bands.1 = (bf16[256,768]{1,0:T(8,128)(2,1)}, bf16[6,128,160]{2,1,0:T(8,128)(2,1)}, bf16[6,256,256]{2,1,0:T(8,128)(2,1)}, bf16[6,256,256]{2,1,0:T(8,128)(2,1)}, ...) custom-call(f32[18,31]{1,0:T(8,128)} %reshape.56.taps_ref), custom_call_target="tpu_custom_call" | custom-call | tf_op jit(solution)/shard_map/bands/pallas_call | solution.py:76
  58.5 10.8 %sides.2.along_ref = bf16[6,32,128,128]{3,2,1,0:T(8,128)(2,1)} custom-call(bf16[32,160,256]{2,1,0:T(8,128)(2,1)} %rim_first.1.wide_ref, bf16[256,768]{1,0:T(8,128)(2,1)} %get-tuple-element.30.bx_ref, bf16[768,160]{1,0:T(8,128)(2,1)} %bitcast.8), custom_call_target="tpu_custom_call" | custom-call | flops 2264924160 | bytes 9437184 | tf_op jit(solution)/shard_map/sides/pallas_call | solution.py:129
  69.3 0.7 broadcast_in_dim.38.count_ref
  70.1 9.3 %weigh.1.weight_ref = f32[6,8,256,256]{3,2,1,0:T(8,128)} custom-call(bf16[6,32,128,128]{3,2,1,0:T(8,128)(2,1)} %sides.2.along_ref, f32[6,32,128]{2,1,0:T(8,128)} %broadcast_in_dim.38.count_ref, bf16[6,256,256]{2,1,0:T(8,128)(2,1)} %get-tuple-element.32.kz_ref), custom_call_target="tpu_custom_call" | custom-call | tf_op jit(solution)/shard_map/weigh/pallas_call | solution.py:170
  79.4 140.4 %all-to-all-done.1 = bf16[32,8,128,128]{3,2,1,0:T(8,128)(2,1)} async-done(((bf16[32,8,128,128]{3,2,1,0:T(8,128)(2,1)}), bf16[32,8,128,128]{3,2,1,0:T(8,128)(2,1)}, u32[]{:S(2)}, u32[]{:S(2)}) %all-to-all-start.1) | async-done | bytes 8388640 | tf_op jit(solution)/shard_map/all_to_all | solution.py:558
  219.8 24.3 %turn.2 = (f32[32,128,128]{2,1,0:T(8,128)}, bf16[32,32,128]{2,1,0:T(8,128)(2,1)}, bf16[4,160,128]{2,1,0:T(8,128)(2,1)}, bf16[4,160,128]{2,1,0:T(8,128)(2,1)}, bf16[6,32,128,128]{3,2,1,0:T(8,128)(2,1)}) custom-call(s32[256]{0:T(256)} %copy-done, bf16[256,128,128]{2,1,0:T(8,128)(2,1)} %bitcast.3.tiles_ref, f32[6,8,256,256]{3,2,1,0:T(8,128)} %weigh.1.weight_ref, ...), custom_call_target="tpu_custom_call" | custom-call | tf_op jit(solution)/shard_map/turn/pallas_call | solution.py:314
  244.1 18.1 %rim_between.1 = (f32[32,128,128]{2,1,0:T(8,128)}, bf16[32,160,256]{2,1,0:T(8,128)(2,1)}) custom-call(f32[32,128,128]{2,1,0:T(8,128)} %est_ref.3, f32[32,128,128]{2,1,0:T(8,128)} %get-tuple-element.36.in_ref, bf16[32,32,128]{2,1,0:T(8,128)(2,1)} %get-tuple-element.37.ys_ref, bf16[4,160,128]{2,1,0:T(8,128)(2,1)} %get-tuple-element.38.xl_ref, ...), custom_call_target="tpu_custom_call" | custom-call | tf_op jit(solution)/shard_map/rim_between/pallas_call | solution.py:519
  262.2 10.8 %sides.3.along_ref = bf16[6,32,128,128]{3,2,1,0:T(8,128)(2,1)} custom-call(bf16[32,160,256]{2,1,0:T(8,128)(2,1)} %get-tuple-element.41.wide_ref, bf16[256,768]{1,0:T(8,128)(2,1)} %get-tuple-element.30.bx_ref, bf16[768,160]{1,0:T(8,128)(2,1)} %bitcast.9), custom_call_target="tpu_custom_call" | custom-call | flops 2264924160 | bytes 9437184 | tf_op jit(solution)/shard_map/sides/pallas_call | solution.py:129
  273.1 16.5 %turn.3 = (f32[32,128,128]{2,1,0:T(8,128)}, bf16[32,32,128]{2,1,0:T(8,128)(2,1)}, bf16[4,160,128]{2,1,0:T(8,128)(2,1)}, bf16[4,160,128]{2,1,0:T(8,128)(2,1)}) custom-call(bf16[6,32,128,128]{3,2,1,0:T(8,128)(2,1)} %sides.3.along_ref, bf16[6,32,128,128]{3,2,1,0:T(8,128)(2,1)} %get-tuple-element.42.seen_ref, f32[6,32,128]{2,1,0:T(8,128)} %broadcast_in_dim.38.count_ref, ...), custom_call_target="tpu_custom_call" | custom-call | tf_op jit(solution)/shard_map/turn/pallas_call | solution.py:314
  289.6 11.9 %rim_last.1 = f32[32,128,128]{2,1,0:T(8,128)} custom-call(f32[32,128,128]{2,1,0:T(8,128)} %get-tuple-element.40.est_ref, f32[32,128,128]{2,1,0:T(8,128)} %get-tuple-element.43.in_ref, bf16[32,32,128]{2,1,0:T(8,128)(2,1)} %get-tuple-element.44.ys_ref, bf16[4,160,128]{2,1,0:T(8,128)(2,1)} %get-tuple-element.45.xl_ref, ...), custom_call_target="tpu_custom_call" | custom-call | tf_op jit(solution)/shard_map/rim_last/pallas_call | solution.py:519
  301.6 3.1 %copy.9 = f32[32,128,128]{2,1,0:T(8,128)} copy(f32[32,128,128]{2,1,0:T(8,128)} %rim_last.1) | data formatting | bytes 4194304
  (1 shorter events, 0.0 us)
Async XLA Ops:
  3.0 25.0 %all-to-all-start = ((s32[32,1,8]{2,1,0:T(1,128)}), s32[32,1,8]{2,1,0:T(1,128)S(1)}, u32[]{:S(2)}, u32[]{:S(2)}) async-start(s32[32,1,8]{2,1,0:T(1,128)} %bitcast.1), calls=%async_computation | async-start | bytes 32768 | tf_op jit(solution)/shard_map/all_to_all | solution.py:551
  29.3 5.0 %copy-start = (s32[256]{0:T(256)}, s32[256]{0:T(256)S(1)}, u32[]{:S(2)}) copy-start(s32[256]{0:T(256)S(1)} %reshape.49.label_ref) | copy-start | bytes 3076
  29.3 5.2 %copy-start.1 = (f32[6,3,31]{2,1,0:T(4,128)S(1)}, f32[6,3,31]{2,1,0:T(4,128)}, u32[]{:S(2)}) copy-start(f32[6,3,31]{2,1,0:T(4,128)} %param.8) | copy-start | bytes 6700
  29.4 190.4 %all-to-all-start.1 = ((bf16[32,8,128,128]{3,2,1,0:T(8,128)(2,1)}), bf16[32,8,128,128]{3,2,1,0:T(8,128)(2,1)}, u32[]{:S(2)}, u32[]{:S(2)}) async-start(bf16[32,8,128,128]{3,2,1,0:T(8,128)(2,1)} %bitcast.7), calls=%async_computation.1 | async-start | bytes 16777216 | tf_op jit(solution)/shard_map/all_to_all | solution.py:558
